TPU v7x, 128 devices: a whole 4x4x4 slice. The times are simulated.
128 devices in a mesh: ctx: 16 (over x_lo, y, core), ch: 8 (over z, x_hi).
Axes of the slice: x: 4 (x_hi: 2, x_lo: 2; x = x_hi * 2 + x_lo), y: 4, z: 4, core: 2. Of those that a mesh axis runs over, the one named last changes fastest.
Arguments:
- hidden: bfloat16 [8192, 4096], P('ctx', 'ch'), may hold values from -6 to 6
- norm_gain: float32 [2, 4096], replicated, may hold values from 0.5 to 2
- in_weight: bfloat16 [2, 4096, 3, 4096], P(None, 'ctx', None, 'ch'), may hold values from -0.09375 to 0.09375
- feat_filter: float32 [2, 3, 3, 4096], P(None, None, None, 'ch'), may hold values from -3 to 3
- se_filter: float32 [7, 4096], P(None, 'ch'), may hold values from -2 to 2
- mr_filter: float32 [128, 4096], P(None, 'ch'), may hold values from -0.5 to 0.5
- skip_gain: float32 [2, 4096], P(None, 'ch'), may hold values from -1 to 1
- out_weight: bfloat16 [2, 4096, 4096], P(None, 'ch', 'ctx'), may hold values from -0.125 to 0.125
Outputs:
- result: bfloat16 [8192, 4096], P('ctx', 'ch')
All inputs are finite; a program needn't handle non-finite values.
Results may differ from a plain program's by a relative error of at most 0.04.
Values may be sent and summed in bfloat16 or wider, within the bound.
No kernel may reach another device: no remote copies, remote signals or barrier semaphores. Data moves between devices by JAX's collectives and lax.ppermute only.
A program may use at most 128 MiB of HBM per device.

v0:
```python
import jax
import jax.numpy as jnp
from jax import lax
from jax.sharding import PartitionSpec as P


def from_behind(value, axis, by):
    devices = lax.axis_size(axis)
    pairs = [(i, i + by) for i in range(devices) if 0 <= i + by < devices]
    return lax.ppermute(value, axis, pairs)


def normalize(whole_rows, gain_row):
    values = whole_rows.astype(jnp.float32)
    inverse_rms = lax.rsqrt(jnp.mean(values * values, axis=-1, keepdims=True) + 1e-06)
    return (values * inverse_rms * gain_row).astype(jnp.bfloat16)


def project_in(normed, weight_shard):
    block_width = weight_shard.shape[0]
    channels = weight_shard.shape[2]
    row_count = normed.shape[0]
    gathered = lax.all_gather(weight_shard, "ctx", axis=0, tiled=True)
    flattened = gathered.reshape(gathered.shape[0], 3 * channels)

    def add_block(block_index, running):
        offset = block_index * block_width
        columns = lax.dynamic_slice_in_dim(normed, offset, block_width, 1)
        weight_rows = lax.dynamic_slice_in_dim(flattened, offset, block_width, 0)
        product = jnp.dot(columns, weight_rows, preferred_element_type=jnp.float32)
        return running + lax.optimization_barrier(product.astype(jnp.bfloat16)).astype(jnp.float32)

    summed = lax.fori_loop(
        0, lax.axis_size("ctx"), add_block, jnp.zeros((row_count, 3 * channels), jnp.float32)
    )
    return summed.astype(jnp.bfloat16).reshape(row_count, 3, channels)


def tail_rows(projected, length):
    channels = projected.shape[2]
    head_rows = projected[-2:, 0]
    pair_rows = projected[-(length + 1) :, 1:].reshape(length + 1, 2 * channels)
    return (head_rows, pair_rows)


def mix_channels(projected, received, shaping, filter_taps, skip_term):
    length = filter_taps.shape[0]
    channels = projected.shape[2]
    head_rows, pair_rows = received
    queries = jnp.concatenate([head_rows, projected[:, 0]], axis=0).astype(jnp.float32)
    key_values = jnp.concatenate(
        [pair_rows.reshape(length + 1, 2, channels), projected[:, 1:]], axis=0
    ).astype(jnp.float32)
    query_shaped = (
        shaping[0, 0] * queries[2:] + shaping[1, 0] * queries[1:-1] + shaping[2, 0] * queries[:-2]
    )
    pair_shaped = (
        shaping[0, 1:] * key_values[2:]
        + shaping[1, 1:] * key_values[1:-1]
        + shaping[2, 1:] * key_values[:-2]
    )
    gated_rows = pair_shaped[:, 0] * pair_shaped[:, 1]
    kernel = filter_taps[::-1][:, None, :]
    filtered = lax.conv_general_dilated(
        gated_rows[None],
        kernel,
        (1,),
        "VALID",
        dimension_numbers=("NWC", "WIO", "NWC"),
        feature_group_count=channels,
        precision=lax.Precision.HIGHEST,
    )[0]
    own_gated = gated_rows[length - 1 :]
    return (query_shaped * (filtered + skip_term * own_gated)).astype(jnp.bfloat16)


def project_out(inner_out, weight_shard):
    return jnp.dot(
        inner_out,
        lax.all_gather(weight_shard, "ctx", axis=1, tiled=True),
        preferred_element_type=jnp.float32,
    )


def per_device(
    hidden, norm_gain, in_weight, feat_filter, se_filter, mr_filter, skip_gain, out_weight
):
    whole_rows = lax.all_gather(hidden, "ch", axis=1, tiled=True)
    projected = project_in(normalize(whole_rows, norm_gain[0]), in_weight[0])
    head_rows, pair_rows = tail_rows(projected, se_filter.shape[0])
    received = from_behind((head_rows, pair_rows), "ctx", 1)
    inner_out = mix_channels(projected, received, feat_filter[0], se_filter, skip_gain[0])
    partial_value = project_out(inner_out, out_weight[0])
    output_sum = lax.psum_scatter(
        partial_value.astype(jnp.bfloat16), "ch", scatter_dimension=1, tiled=True
    ).astype(jnp.float32)
    current = (hidden.astype(jnp.float32) + output_sum).astype(jnp.bfloat16)
    whole_rows = lax.all_gather(current, "ch", axis=1, tiled=True)
    projected = project_in(normalize(whole_rows, norm_gain[1]), in_weight[1])
    head_rows, pair_rows = tail_rows(projected, mr_filter.shape[0])
    received = from_behind((head_rows, pair_rows), "ctx", 1)
    inner_out = mix_channels(projected, received, feat_filter[1], mr_filter, skip_gain[1])
    partial_value = project_out(inner_out, out_weight[1])
    output_sum = lax.psum_scatter(
        partial_value.astype(jnp.bfloat16), "ch", scatter_dimension=1, tiled=True
    ).astype(jnp.float32)
    return (current.astype(jnp.float32) + output_sum).astype(jnp.bfloat16)


def solution(mesh):
    return jax.shard_map(
        per_device,
        mesh=mesh,
        in_specs=(
            P("ctx", "ch"),
            P(),
            P(None, "ctx", None, "ch"),
            P(None, None, None, "ch"),
            P(None, "ch"),
            P(None, "ch"),
            P(None, "ch"),
            P(None, "ch", "ctx"),
        ),
        out_specs=P("ctx", "ch"),
        check_vma=False,
    )
```

profile of v0, /device:TPU:1, one launch (start us, length us, event | category | flops | bytes accessed | tf_op | source)
XLA Modules:
  0.0 757.1 jit_solution(9231638023574212701)
XLA Ops:
  11.4 74.8 %all-gather.11.cloned.1.call-done = bf16[512,4096]{1,0:T(8,128)(2,1)} async-done(((bf16[512,512]{1,0:T(8,128)(2,1)}), bf16[512,4096]{1,0:T(8,128)(2,1)}) %all-gather.11.cloned.1.call-update) | async-done | bytes 4194320 | tf_op jit(solution)/shard_map/all_gather | solution.py:88
  86.2 3.2 fusion.6
  89.7 3.6 fusion.8
  93.3 72.5 %all-gather.15.cloned.1.call-done = bf16[1,4096,3,512]{1,3,2,0:T(8,128)(2,1)} async-done(((bf16[1,256,3,512]{1,3,2,0:T(8,128)(2,1)}), bf16[1,4096,3,512]{1,3,2,0:T(8,128)(2,1)}) %all-gather.15.cloned.1.call-update) | async-done | bytes 12582928 | tf_op jit(solution)/shard_map/all_gather | solution.py:23
  165.8 92.1 %while.28 = (s32[]{:T(128)}, f32[512,1536]{1,0:T(8,128)}, bf16[512,4096]{1,0:T(8,128)(2,1)}, bf16[4096,1536]{0,1:T(8,128)(2,1)}, s32[]{:T(128)}, /*index=5*/s32[]{:T(128)}, s32[]{:T(128)}, s32[]{:T(128)}) while((s32[]{:T(128)}, f32[512,1536]{1,0:T(8,128)}, bf16[512,4096]{1,0:T(8,128)(2,1)}, bf16[4096,1536]{0,1:T(8,128)(2,1)}, ...), condition=%wide.region_2.0_spmd.clone, body=%wide.region_1.0_spmd.clone.sunk | while | flops 405798912 | bytes 10486925 | solution.py:33
  171.6 4.0 select_add_fusion.4
  177.6 4.0 select_add_fusion.4
  183.4 4.0 select_add_fusion.4
  189.3 4.0 select_add_fusion.4
  195.2 4.1 select_add_fusion.4
  201.1 4.1 select_add_fusion.4
  207.0 4.1 select_add_fusion.4
  212.9 4.0 select_add_fusion.4
  218.8 4.0 select_add_fusion.4
  224.6 4.0 select_add_fusion.4
  230.5 4.0 select_add_fusion.4
  236.3 4.0 select_add_fusion.4
  242.2 4.0 select_add_fusion.4
  248.0 4.0 select_add_fusion.4
  253.9 4.0 select_add_fusion.4
  272.4 3.7 copy.48
  280.2 2.8 copy.35
  283.0 2.8 reshape.110
  287.0 9.3 %convolution_convert_fusion.3 = bf16[512,4096]{1,0:T(8,128)(2,1)} fusion(bf16[1,512,4096]{2,1,0:T(8,128)(2,1)} %all-gather.17.cloned.1.call-done, f32[518,1,512]{0,2,1:T(8,128)} %slice_multiply_fusion.7, f32[1,520,512]{1,2,0:T(8,128)} %reshape.110, f32[514,512]{0,1:T(8,128)} %maximum_convert_fusion.2, f32[512]{0:T(512)S(1)} %bitcast.108, ...), kind=kOutput, calls=%fused_computation.21 | convolution fusion | flops 2151940096 | bytes 13639680 | tf_op jit(solution)/shard_map/dot_general | solution.py:78
  296.4 85.7 %reduce-scatter.3.cloned.1.call-done = bf16[512,512]{1,0:T(8,128)(2,1)} async-done(((bf16[512,4096]{1,0:T(8,128)(2,1)}), bf16[512,512]{1,0:T(8,128)(2,1)}) %reduce-scatter.3.cloned.1.call-update) | async-done | bytes 524304 | tf_op jit(solution)/shard_map/reduce_scatter | solution.py:94
  386.4 71.1 %all-gather.13.cloned.1.call-done = bf16[512,4096]{1,0:T(8,128)(2,1)} async-done(((bf16[512,512]{1,0:T(8,128)(2,1)}), bf16[512,4096]{1,0:T(8,128)(2,1)}) %all-gather.13.cloned.1.call-update) | async-done | bytes 4194320 | tf_op jit(solution)/shard_map/all_gather | solution.py:98
  457.5 3.2 fusion.9
  460.9 3.6 fusion.11
  464.5 72.5 %all-gather.19.cloned.1.call-done = bf16[1,4096,3,512]{1,3,2,0:T(8,128)(2,1)} async-done(((bf16[1,256,3,512]{1,3,2,0:T(8,128)(2,1)}), bf16[1,4096,3,512]{1,3,2,0:T(8,128)(2,1)}) %all-gather.19.cloned.1.call-update) | async-done | bytes 12582928 | tf_op jit(solution)/shard_map/all_gather | solution.py:23
  537.0 92.1 %while.29 = (s32[]{:T(128)}, f32[512,1536]{1,0:T(8,128)}, bf16[512,4096]{1,0:T(8,128)(2,1)}, bf16[4096,1536]{0,1:T(8,128)(2,1)}, s32[]{:T(128)}, /*index=5*/s32[]{:T(128)}, s32[]{:T(128)}, s32[]{:T(128)}) while((s32[]{:T(128)}, f32[512,1536]{1,0:T(8,128)}, bf16[512,4096]{1,0:T(8,128)(2,1)}, bf16[4096,1536]{0,1:T(8,128)(2,1)}, ...), condition=%wide.region_6.0_spmd.clone, body=%wide.region_5.0_spmd.clone.sunk | while | flops 405798912 | bytes 10486925 | solution.py:33
  542.8 4.0 select_add_fusion.5
  548.8 4.0 select_add_fusion.5
  554.7 4.0 select_add_fusion.5
  560.5 4.0 select_add_fusion.5
  566.4 4.1 select_add_fusion.5
  572.3 4.1 select_add_fusion.5
  578.3 4.1 select_add_fusion.5
  584.2 4.0 select_add_fusion.5
  590.0 4.0 select_add_fusion.5
  595.9 4.0 select_add_fusion.5
  601.7 4.0 select_add_fusion.5
  607.6 4.0 select_add_fusion.5
  613.4 4.0 select_add_fusion.5
  619.3 4.0 select_add_fusion.5
  625.1 4.0 select_add_fusion.5
  643.6 11.9 %fusion.18 = f32[1,512,512]{2,0,1:T(1,128)} fusion(f32[1,639,512]{2,1,0:T(8,128)S(1)} %fusion.60, f32[128,1,512]{2,0,1:T(8,128)S(1)} %bitcast.100), kind=kOutput, calls=%fused_computation.39 | convolution fusion | flops 402653184 | bytes 2619392 | tf_op jit(solution)/shard_map/conv_general_dilated | solution.py:64
  655.5 7.1 convolution_convert_fusion.2
  662.7 85.6 %reduce-scatter.5.cloned.1.call-done = bf16[512,512]{1,0:T(8,128)(2,1)} async-done(((bf16[512,4096]{1,0:T(8,128)(2,1)}), bf16[512,512]{1,0:T(8,128)(2,1)}) %reduce-scatter.5.cloned.1.call-update) | async-done | bytes 524304 | tf_op jit(solution)/shard_map/reduce_scatter | solution.py:104
  (134 shorter events, 108.4 us)
Async XLA Ops:
  6.5 79.7 %all-gather.11.cloned.1.call-start = ((), (), s32[]{:S(2)}) async-start(), calls=%async_computation.2 | async-start | bytes 4718592 | tf_op jit(solution)/shard_map/all_gather | solution.py:88
  7.3 3.0 copy-start.4
  7.3 158.5 %all-gather.15.cloned.1.call-start = ((), (), s32[]{:S(2)}) async-start(), calls=%async_computation.6 | async-start | bytes 13369344 | tf_op jit(solution)/shard_map/all_gather | solution.py:23
  8.8 2.3 copy-start.7
  8.8 2.4 copy-start.8
  8.9 2.4 copy-start.9
  8.9 2.5 copy-start.10
  10.2 276.9 %all-gather.17.cloned.1.call-start = ((), (), s32[]{:S(2)}) async-start(), calls=%async_computation.7 | async-start | bytes 4456448 | tf_op jit(solution)/shard_map/all_gather | solution.py:80
  11.1 371.0 %reduce-scatter.3.cloned.1.call-start = ((), (), s32[]{:S(2)}) async-start(), calls=%async_computation.3 | async-start | bytes 4718592 | tf_op jit(solution)/shard_map/reduce_scatter | solution.py:94
  86.2 3.4 copy-start
  260.2 5.1 collective-permute-start
  263.1 5.2 collective-permute-start.1
  276.1 2.1 copy-start.11
  296.3 85.7 %copy-start.3 = (bf16[512,512]{1,0:T(8,128)(2,1)S(1)}, bf16[512,512]{1,0:T(8,128)(2,1)}, u32[]{:S(2)}) copy-start(bf16[512,512]{1,0:T(8,128)(2,1)} %param.12) | copy-start | bytes 1572868
  296.4 161.1 %all-gather.13.cloned.1.call-start = ((), (), s32[]{:S(2)}) async-start(), calls=%async_computation.4 | async-start | bytes 4718592 | tf_op jit(solution)/shard_map/all_gather | solution.py:98
  384.1 153.0 %all-gather.19.cloned.1.call-start = ((), (), s32[]{:S(2)}) async-start(), calls=%async_computation.8 | async-start | bytes 13369344 | tf_op jit(solution)/shard_map/all_gather | solution.py:23
  385.4 270.2 %all-gather.21.cloned.1.call-start = ((), (), s32[]{:S(2)}) async-start(), calls=%async_computation.9 | async-start | bytes 4456448 | tf_op jit(solution)/shard_map/all_gather | solution.py:80
  386.1 362.2 %reduce-scatter.5.cloned.1.call-start = ((), (), s32[]{:S(2)}) async-start(), calls=%async_computation.5 | async-start | bytes 4718592 | tf_op jit(solution)/shard_map/reduce_scatter | solution.py:104
  457.5 3.4 copy-start.1
  629.1 7.5 copy-start.5
  631.8 7.0 collective-permute-start.2
  634.7 5.4 collective-permute-start.3
  642.7 1.0 copy-start.6
  662.7 85.7 %copy-start.2 = (bf16[512,512]{1,0:T(8,128)(2,1)S(1)}, bf16[512,512]{1,0:T(8,128)(2,1)}, u32[]{:S(2)}) copy-start(bf16[512,512]{1,0:T(8,128)(2,1)} %add_convert_fusion.1) | copy-start | bytes 1572868
Sparse Core Ops, SparseCore 0:
  9.5 76.6 all-gather.10
  87.8 77.9 all-gather.14
  167.4 45.1 all-gather.16
  296.5 85.5 reduce-scatter.2
  384.3 73.1 all-gather.12
  459.0 77.9 all-gather.18
  538.7 45.1 all-gather.20
  662.8 85.4 reduce-scatter.4
where the time goes:
time: 760 us; the launch traced here: 757 us
  waiting for transfers between devices  466 us (61%)
  other arithmetic  151 us (20%)
  matrix products  88.9 us (12%)
  local copies, waits for them, and re-layouts  26.3 us (3%)
  between operations  13.9 us (2%)
  starting transfers between devices  9.89 us (1%)
    reduce_scatter x2, waiting for transfers between devices, per_device(): lax.psum_scatter(partial_value.astype(jnp.bfloat16), 'ch', scatter_dimens...  171 us
    all_gather x2, waiting for transfers between devices, project_in(): gathered = lax.all_gather(weight_shard, 'ctx', axis=0, tiled=True)  145 us
    add x32, other arithmetic, add_block(): running + lax.optimization_barrier(product.astype(jnp.bfloat16)).astype(j...  125 us
    all_gather x1, waiting for transfers between devices, per_device(): whole_rows = lax.all_gather(hidden, 'ch', axis=1, tiled=True)  74.8 us
    all_gather x1, waiting for transfers between devices, per_device(): whole_rows = lax.all_gather(current, 'ch', axis=1, tiled=True)  71.1 us
    dot_general x32, matrix products, add_block(): product = jnp.dot(columns, weight_rows, preferred_element_type=jnp.float32)  58.6 us
    dot_general x2, matrix products, project_out(): jnp.dot(inner_out, lax.all_gather(weight_shard, 'ctx', axis=1, tiled=True...  16.4 us
  transfers between devices with their start and end apart: 12, of which 8 were waited for; matrix products, arithmetic and copies ran while one was open for 32% of the time, Pallas kernels for 0%

commit v1 on v0

v1 whole, which is shorter than its diff:
```python
import jax
import jax.numpy as jnp
import numpy as np
from jax import lax
from jax.sharding import Mesh, PartitionSpec as P

AXES = ("xl", "y", "core", "z", "xh")


def shift(value, axis, by):
    size = lax.axis_size(axis)
    return lax.ppermute(value, axis, [(i, (i + by) % size) for i in range(size)])


def swap(value):
    moved = lax.ppermute(value, ("core", "xh"), [(1, 2), (2, 1)])
    same = lax.axis_index("core") == lax.axis_index("xh")
    return jnp.where(same, value, moved)


def behind(value, axes):
    size = 16
    return lax.ppermute(value, axes, [(i, i + 1) for i in range(size - 1)])


def around(value, axis="z"):
    return [value, shift(value, axis, 1), shift(value, axis, 2), shift(value, axis, -1)]


def in_order(pieces, me):
    stacked = jnp.stack(pieces)
    return [lax.dynamic_index_in_dim(stacked, (me - i) % len(pieces), 0, keepdims=False) for i in range(len(pieces))]


def normalize(whole_rows, gain_row):
    values = whole_rows.astype(jnp.float32)
    inverse_rms = lax.rsqrt(jnp.mean(values * values, axis=-1, keepdims=True) + 1e-06)
    return (values * inverse_rms * gain_row).astype(jnp.bfloat16)


def mix_channels(projected, axes, shaping, filter_taps, skip_term):
    length = filter_taps.shape[0]
    channels = projected.shape[2]
    head_rows, pair_rows = behind((projected[-2:, 0], projected[-(length + 1) :, 1:].reshape(length + 1, 2 * channels)), axes)
    queries = jnp.concatenate([head_rows, projected[:, 0]], axis=0).astype(jnp.float32)
    key_values = jnp.concatenate(
        [pair_rows.reshape(length + 1, 2, channels), projected[:, 1:]], axis=0
    ).astype(jnp.float32)
    query_shaped = shaping[0, 0] * queries[2:] + shaping[1, 0] * queries[1:-1] + shaping[2, 0] * queries[:-2]
    pair_shaped = (
        shaping[0, 1:] * key_values[2:] + shaping[1, 1:] * key_values[1:-1] + shaping[2, 1:] * key_values[:-2]
    )
    gated_rows = pair_shaped[:, 0] * pair_shaped[:, 1]
    rows = projected.shape[0]
    if length < 16:
        filtered = sum(filter_taps[j] * gated_rows[length - 1 - j : length - 1 - j + rows] for j in range(length))
    else:
        filtered = lax.conv_general_dilated(
            gated_rows[None],
            filter_taps[::-1][:, None, :],
            (1,),
            "VALID",
            dimension_numbers=("NWC", "WIO", "NWC"),
            feature_group_count=channels,
            precision=lax.Precision.HIGHEST,
        )[0]
    own_gated = gated_rows[length - 1 :]
    return (query_shaped * (filtered + skip_term * own_gated)).astype(jnp.bfloat16)


def per_device(hidden, norm_gain, in_weight, feat_filter, se_filter, mr_filter, skip_gain, out_weight):
    z = lax.axis_index("z")
    core = lax.axis_index("core")
    xh = lax.axis_index("xh")
    rows = hidden.shape[0]

    w0 = lax.all_gather(in_weight[0].reshape(256, 1536), ("xl", "y", "core"), axis=0, tiled=True)
    mine = out_weight[0]
    both = in_order([mine, shift(mine, "xl", 1)], lax.axis_index("xl"))
    both = jnp.stack(both)
    lines = around(both, "y")
    other = [shift(v, "core", 1) for v in lines]
    lines = jnp.stack(in_order(lines, lax.axis_index("y")))
    other = jnp.stack(in_order(other, lax.axis_index("y")))
    pair = jnp.stack([lines, other])
    pair = jnp.where(core == 0, pair, pair[::-1])
    o0 = pair.transpose(3, 2, 1, 0, 4).reshape(512, 4096)

    w1_mine = swap(in_weight[1].reshape(256, 1536))
    o1_mine = swap(out_weight[1])
    small = swap(jnp.concatenate([feat_filter[1].reshape(9, 512), skip_gain[1:2], mr_filter], axis=0))

    duo = jnp.concatenate(in_order([hidden, shift(hidden, "xh", 1)], xh), axis=1)
    whole = jnp.concatenate(in_order(around(duo), z), axis=1)
    normed = normalize(whole, norm_gain[0])
    projected = jnp.dot(normed, w0, preferred_element_type=jnp.float32).astype(jnp.bfloat16).reshape(rows, 3, 512)
    inner = mix_channels(projected, ("xl", "y", "core"), feat_filter[0], se_filter, skip_gain[0])
    part = jnp.dot(inner, o0, preferred_element_type=jnp.float32).astype(jnp.bfloat16)

    def for_z(array, by):
        return lax.dynamic_slice_in_dim(array, ((z + by) % 4) * 1024, 1024, 1)

    total = for_z(part, 0).astype(jnp.float32)
    for by in (1, -1, 2):
        total = total + shift(for_z(part, by), "z", by).astype(jnp.float32)
    total = total.astype(jnp.bfloat16)
    halves = [total[:, :512], total[:, 512:]]
    pick = lambda c: jnp.where(c == 0, halves[0], halves[1])
    first = lax.ppermute(pick(core), ("core", "xh"), [(1, 0), (2, 3)])
    second = lax.ppermute(pick(1 - core), ("core", "xh"), [(1, 2), (2, 1)])
    third = lax.ppermute(pick(1 - core), ("core", "xh"), [(0, 2), (3, 1)])
    base = swap(hidden)
    kept = jnp.where(core == xh, pick(core), jnp.zeros_like(first))
    current = (
        base.astype(jnp.float32)
        + kept.astype(jnp.float32)
        + first.astype(jnp.float32)
        + second.astype(jnp.float32)
        + third.astype(jnp.float32)
    ).astype(jnp.bfloat16)

    w1 = lax.all_gather(w1_mine, ("xh", "xl", "y"), axis=0, tiled=False)
    w1 = w1.reshape(2, 8, 256, 1536).transpose(1, 0, 2, 3).reshape(4096, 1536)
    o1 = lax.all_gather(o1_mine, ("xh", "xl", "y"), axis=0, tiled=False)
    o1 = o1.reshape(2, 8, 512, 256).transpose(2, 1, 0, 3).reshape(512, 4096)
    near = around(current)
    far = [shift(v, "core", 1) for v in near]
    near, far = jnp.stack(in_order(near, z)), jnp.stack(in_order(far, z))
    by_core = jnp.stack([near, far])
    by_core = jnp.where(core == 0, by_core, by_core[::-1])
    whole = by_core.transpose(2, 1, 0, 3).reshape(rows, 4096)
    normed = normalize(whole, norm_gain[1])
    projected = jnp.dot(normed, w1, preferred_element_type=jnp.float32).astype(jnp.bfloat16).reshape(rows, 3, 512)
    inner = mix_channels(projected, ("xl", "y", "xh"), small[:9].reshape(3, 3, 512), small[10:], small[9])
    part = jnp.dot(inner, o1, preferred_element_type=jnp.float32).astype(jnp.bfloat16)
    part = part.reshape(rows, 4, 2, 512).transpose(2, 1, 0, 3)
    own = jnp.where(core == 0, part[0], part[1])
    theirs = jnp.where(core == 0, part[1], part[0])
    both = (own.astype(jnp.float32) + shift(theirs, "core", 1).astype(jnp.float32)).astype(jnp.bfloat16)
    block = lambda by: lax.dynamic_index_in_dim(both, (z + by) % 4, 0, keepdims=False)
    total = current.astype(jnp.float32) + block(0).astype(jnp.float32)
    for by in (1, -1, 2):
        total = total + shift(block(by), "z", by).astype(jnp.float32)
    return swap(total.astype(jnp.bfloat16))


def solution(mesh):
    fine = Mesh(np.asarray(mesh.devices).reshape(2, 4, 2, 4, 2), AXES)
    ctx, ch = ("xl", "y", "core"), ("z", "xh")
    return jax.shard_map(
        per_device,
        mesh=fine,
        in_specs=(
            P(ctx, ch),
            P(),
            P(None, ctx, None, ch),
            P(None, None, None, ch),
            P(None, ch),
            P(None, ch),
            P(None, ch),
            P(None, ch, ctx),
        ),
        out_specs=P(ctx, ch),
        check_vma=False,
    )
```

time: 760 us -> 488 us (0.64)
  the two profiles are of different devices: /device:TPU:1 before, /device:TPU:11 now
where the time goes in v1:
time: 488 us; the launch traced here: 481 us
  waiting for transfers between devices  168 us (34%)
  starting transfers between devices  141 us (29%)
  local copies, waits for them, and re-layouts  74.7 us (15%)
  matrix products  46.5 us (10%)
  other arithmetic  36.7 us (8%)
  between operations  14.7 us (3%)
    ppermute x26, waiting for transfers between devices, shift(): lax.ppermute(value, axis, [(i, (i + by) % size) for i in range(size)])  130 us
    ppermute x26, starting transfers between devices, shift(): lax.ppermute(value, axis, [(i, (i + by) % size) for i in range(size)])  69.6 us
    ppermute x4, starting transfers between devices, behind(): return lax.ppermute(value, axes, [(i, i + 1) for i in range(size - 1)])  42.5 us
    ppermute x5, starting transfers between devices, swap(): moved = lax.ppermute(value, ('core', 'xh'), [(1, 2), (2, 1)])  21.8 us
    ppermute x5, waiting for transfers between devices, swap(): moved = lax.ppermute(value, ('core', 'xh'), [(1, 2), (2, 1)])  18.3 us
    unnamed x36, local copies, waits for them, and re-layouts  18.1 us
    reshape x1, local copies, waits for them, and re-layouts, per_device(): w1 = w1.reshape(2, 8, 256, 1536).transpose(1, 0, 2, 3).reshape(4096, 1536)  16.8 us
    dot_general x1, matrix products, per_device(): jnp.dot(normed, w0, preferred_element_type=jnp.float32).astype(jnp.bfloat16)  13 us
  transfers between devices with their start and end apart: 41, of which 20 were waited for; matrix products, arithmetic and copies ran while one was open for 23% of the time, Pallas kernels for 0%

profile of v1, /device:TPU:11, one launch (start us, length us, event | category | flops | bytes accessed | tf_op | source)
XLA Modules:
  0.0 481.2 jit_solution(7703471490271556783)
XLA Ops:
  9.5 4.3 collective-permute-start.29
  13.9 10.5 %collective-permute-done.29 = bf16[256,1536]{0,1:T(8,128)(2,1)S(1)} collective-permute-done((bf16[256,1536]{0,1:T(8,128)(2,1)S(1)}, bf16[256,1536]{0,1:T(8,128)(2,1)S(1)}, u32[]{:S(2)}, u32[]{:S(2)}) %collective-permute-start.29) | collective-permute-done | bytes 786464 | tf_op jit(solution)/shard_map/ppermute | solution.py:16
  26.2 4.8 collective-permute-start.32
  31.1 9.1 %collective-permute-done.7 = bf16[512,256]{0,1:T(8,128)(2,1)S(1)} collective-permute-done((bf16[512,256]{0,1:T(8,128)(2,1)S(1)}, bf16[512,256]{0,1:T(8,128)(2,1)S(1)}, u32[]{:S(2)}, u32[]{:S(2)}) %collective-permute-start.7) | collective-permute-done | bytes 262176 | tf_op jit(solution)/shard_map/ppermute | solution.py:12
  41.8 24.4 %collective-permute-start.9 = (bf16[2,512,256]{1,2,0:T(8,128)(2,1)S(1)}, bf16[2,512,256]{1,2,0:T(8,128)(2,1)}, u32[]{:S(2)}, u32[]{:S(2)}) collective-permute-start(bf16[2,512,256]{1,2,0:T(8,128)(2,1)S(1)} %get-tuple-element.40), channel_id=1, source_target_pairs={{0,32},{16,48},{32,0},{48,16},{1,33},{17,49},{33,1},{49,17},{2,34}... | collective-permute-start | bytes 1572872 | tf_op jit(solution)/shard_map/ppermute | solution.py:12
  66.7 8.7 %collective-permute-start.11 = (bf16[2,512,256]{1,2,0:T(8,128)(2,1)S(1)}, bf16[2,512,256]{1,2,0:T(8,128)(2,1)S(1)}, u32[]{:S(2)}, u32[]{:S(2)}) collective-permute-start(bf16[2,512,256]{1,2,0:T(8,128)(2,1)S(1)} %get-tuple-element.40), channel_id=1, source_target_pairs={{0,8},{8,0},{1,9},{9,1},{2,10},{10,2},{3,11},{11,3},{4,12},{12,4},... | collective-permute-start | bytes 1572872 | tf_op jit(solution)/shard_map/ppermute | solution.py:12
  75.3 3.6 collective-permute-done.8
  78.9 16.3 %collective-permute-start.12 = (bf16[2,512,256]{1,2,0:T(8,128)(2,1)}, bf16[2,512,256]{1,2,0:T(8,128)(2,1)S(1)}, u32[]{:S(2)}, u32[]{:S(2)}) collective-permute-start(bf16[2,512,256]{1,2,0:T(8,128)(2,1)} %collective-permute-done.8), channel_id=1, source_target_pairs={{0,8},{8,0},{1,9},{9,1},{2,10},{10,2},{3,11},{11,3},{4,12},{12,4},... | collective-permute-start | bytes 1572872 | tf_op jit(solution)/shard_map/ppermute | solution.py:12
  96.6 3.7 collective-permute-done.10
  100.3 2.9 collective-permute-start.14
  106.1 2.1 collective-permute-start.3
  110.9 3.1 reverse_select_fusion.1
  114.0 18.0 %collective-permute-done.2 = bf16[512,1024]{1,0:T(8,128)(2,1)S(1)} collective-permute-done((bf16[512,1024]{1,0:T(8,128)(2,1)S(1)}, bf16[512,1024]{1,0:T(8,128)(2,1)S(1)}, u32[]{:S(2)}, u32[]{:S(2)}) %collective-permute-start.2) | collective-permute-done | bytes 1048608 | tf_op jit(solution)/shard_map/ppermute | solution.py:12
  131.9 22.1 %collective-permute-done.3 = bf16[512,1024]{1,0:T(8,128)(2,1)S(1)} collective-permute-done((bf16[512,1024]{1,0:T(8,128)(2,1)S(1)}, bf16[512,1024]{1,0:T(8,128)(2,1)S(1)}, u32[]{:S(2)}, u32[]{:S(2)}) %collective-permute-start.3) | collective-permute-done | bytes 1048608 | tf_op jit(solution)/shard_map/ppermute | solution.py:12
  157.6 13.0 %fusion.12 = bf16[512,1536]{1,0:T(8,128)(2,1)} fusion(bf16[4096,1536]{0,1:T(8,128)(2,1)} %all-gather.6.cloned.1.call-done, f32[4096]{0:T(1024)S(1)} %bitcast.269, f32[512]{0:T(512)S(1)} %add_rsqrt_fusion.1, bf16[512,1024]{1,0:T(8,128)(2,1)S(1)} %get-tuple-element.9, bf16[512,1024]{1,0:T(8,128)(2,1)S(1)} %get-tuple-element.10, ...), kind=kOutput, calls=%fused_computation.25 | convolution fusion | flops 6466306048 | bytes 18368512 | tf_op jit(solution)/shard_map/dot_general | solution.py:96
  172.5 19.9 %collective-permute-start.5 = (bf16[2,512]{0,1:T(8,128)(2,1)S(1)}, bf16[2,512]{0,1:T(8,128)(2,1)S(1)}, u32[]{:S(2)}, u32[]{:S(2)}) collective-permute-start(bf16[2,512]{0,1:T(8,128)(2,1)S(1)} %slice_bitcast_fusion.10), channel_id=1, source_target_pairs={{0,8},{8,16},{16,24},{24,32},{32,40},{40,48},{48,56},{56,64},{64,7... | collective-permute-start | bytes 6152 | tf_op jit(solution)/shard_map/ppermute | solution.py:23
  196.9 8.1 %collective-permute-done.6 = bf16[8,1024]{0,1:T(8,128)(2,1)S(1)} collective-permute-done((bf16[8,1024]{0,1:T(8,128)(2,1)S(1)}, bf16[8,1024]{0,1:T(8,128)(2,1)S(1)}, u32[]{:S(2)}, u32[]{:S(2)}) %collective-permute-start.6) | collective-permute-done | bytes 16416 | tf_op jit(solution)/shard_map/ppermute | solution.py:23
  205.6 2.3 fusion.17
  208.0 5.7 %convolution_convert_fusion.1 = bf16[512,4096]{1,0:T(8,128)(2,1)S(1)} fusion(bf16[512,4096]{0,1:T(8,128)(2,1)S(1)} %bitcast.242, f32[518,1,512]{0,2,1:T(8,128)S(1)} %slice_multiply_fusion.7, f32[514,512]{0,1:T(8,128)S(1)} %maximum_convert_fusion.2, f32[512]{0:T(512)S(1)} %bitcast.282, f32[512]{0:T(512)S(1)} %bitcast.276, f32[512]{0:T(512)S(1)} %bitcast.277, ...), kind=kOutput, calls=%fused_computation.14 | convolution fusion | flops 2155347968 | bytes 18896896 | tf_op jit(solution)/shard_map/dot_general | solution.py:98
  216.4 2.7 collective-permute-start.16
  222.8 17.9 %collective-permute-done.15 = bf16[512,1024]{1,0:T(8,128)(2,1)S(1)} collective-permute-done((bf16[512,1024]{1,0:T(8,128)(2,1)}, bf16[512,1024]{1,0:T(8,128)(2,1)S(1)}, u32[]{:S(2)}, u32[]{:S(2)}) %collective-permute-start.15) | collective-permute-done | bytes 1048608 | tf_op jit(solution)/shard_map/ppermute | solution.py:12
  242.0 16.2 %collective-permute-done.17 = bf16[512,1024]{1,0:T(8,128)(2,1)} collective-permute-done((bf16[512,1024]{1,0:T(8,128)(2,1)S(1)}, bf16[512,1024]{1,0:T(8,128)(2,1)}, u32[]{:S(2)}, u32[]{:S(2)}) %collective-permute-start.17) | collective-permute-done | bytes 1048608 | tf_op jit(solution)/shard_map/ppermute | solution.py:12
  258.2 2.8 add_convert_fusion
  261.1 3.4 collective-permute-start.18
  267.7 2.8 collective-permute-done.18
  270.5 7.1 %collective-permute-done.19 = bf16[512,512]{1,0:T(8,128)(2,1)S(1)} collective-permute-done((bf16[512,512]{1,0:T(8,128)(2,1)S(1)}, bf16[512,512]{1,0:T(8,128)(2,1)S(1)}, u32[]{:S(2)}, u32[]{:S(2)}) %collective-permute-start.19) | collective-permute-done | bytes 524320 | tf_op jit(solution)/shard_map/ppermute | solution.py:110
  281.5 6.5 %collective-permute-start.21 = (f32[138,512]{1,0:T(8,128)S(1)}, f32[138,512]{1,0:T(8,128)}, u32[]{:S(2)}, u32[]{:S(2)}) collective-permute-start(f32[138,512]{1,0:T(8,128)S(1)} %pad_maximum_fusion.11), channel_id=1, source_target_pairs={{1,8},{8,1},{3,10},{10,3},{5,12},{12,5},{7,14},{14,7},{17,24},{24,... | collective-permute-start | bytes 847880 | tf_op jit(solution)/shard_map/ppermute | solution.py:16
  288.1 9.8 %collective-permute-done.22 = bf16[512,512]{1,0:T(8,128)(2,1)S(1)} collective-permute-done((bf16[512,512]{1,0:T(8,128)(2,1)S(1)}, bf16[512,512]{1,0:T(8,128)(2,1)S(1)}, u32[]{:S(2)}, u32[]{:S(2)}) %collective-permute-start.22) | collective-permute-done | bytes 524320 | tf_op jit(solution)/shard_map/ppermute | solution.py:12
  299.8 12.0 %copy.75 = bf16[192,8,16,256]{3,2,1,0:T(8,128)(2,1)} copy(bf16[192,8,16,256]{3,1,2,0:T(8,128)(2,1)} %bitcast.230) | data formatting | bytes 25165824
  311.8 16.8 %copy.54 = bf16[2,8,256,1536]{3,2,0,1:T(8,128)(2,1)} copy(bf16[2,8,256,1536]{2,1,0,3:T(8,128)(2,1)} %bitcast.226) | data formatting | bytes 25165824 | tf_op jit(solution)/shard_map/reshape | solution.py:123
  333.0 3.6 fusion.6
  336.6 7.3 %copy.52 = bf16[512,4,2,512]{0,3,2,1:T(8,128)(2,1)} copy(bf16[512,4,2,512]{3,0,1,2:T(8,128)(2,1)} %fusion.6) | data formatting | bytes 8388608 | tf_op jit(solution)/shard_map/convert_element_type | solution.py:38
  343.9 11.9 %convolution_convert_fusion.2 = bf16[512,1536]{1,0:T(8,128)(2,1)} fusion(bf16[512,4096]{0,1:T(8,128)(2,1)} %bitcast.244, bf16[4096,1536]{1,0:T(8,128)(2,1)} %bitcast.231), kind=kOutput, calls=%fused_computation.24 | convolution fusion | flops 6443237376 | bytes 18350080 | tf_op jit(solution)/shard_map/dot_general | solution.py:133
  358.1 5.0 %collective-permute-start.31 = (bf16[129,1024]{1,0:T(8,128)(2,1)S(1)}, bf16[129,1024]{1,0:T(8,128)(2,1)}, u32[]{:S(2)}, u32[]{:S(2)}) collective-permute-start(bf16[129,1024]{1,0:T(8,128)(2,1)S(1)} %copy.58), channel_id=1, source_target_pairs={{0,1},{1,16},{16,17},{17,32},{32,33},{33,48},{48,49},{49,64},{64,6... | collective-permute-start | bytes 792584 | tf_op jit(solution)/shard_map/ppermute | solution.py:23
  363.1 15.5 %collective-permute-start.30 = (bf16[2,512]{1,0:T(2,128)(2,1)S(1)}, bf16[2,512]{1,0:T(2,128)(2,1)S(1)}, u32[]{:S(2)}, u32[]{:S(2)}) collective-permute-start(bf16[2,512]{1,0:T(2,128)(2,1)S(1)} %bitcast.270), channel_id=1, source_target_pairs={{0,1},{1,16},{16,17},{17,32},{32,33},{33,48},{48,49},{49,64},{64,6... | collective-permute-start | bytes 6152 | tf_op jit(solution)/shard_map/ppermute | solution.py:23
  380.1 6.5 %copy.63 = bf16[512,8,2,256]{0,3,2,1:T(8,128)(2,1)} copy(bf16[512,8,2,256]{3,0,1,2:T(8,128)(2,1)} %bitcast.241) | data formatting | bytes 8388608 | tf_op jit(solution)/shard_map/transpose | solution.py:125
  393.0 11.2 %fusion.19 = f32[1,512,512]{2,0,1:T(1,128)S(1)} fusion(f32[1,639,512]{2,1,0:T(8,128)S(1)} %fusion.87, f32[128,1,512]{2,0,1:T(8,128)S(1)} %bitcast.264), kind=kOutput, calls=%fused_computation.50 | convolution fusion | flops 402653184 | bytes 2619392 | tf_op jit(solution)/shard_map/conv_general_dilated | solution.py:58
  404.2 4.6 convolution_convert_fusion
  408.8 6.5 %copy.64 = bf16[512,4096]{0,1:T(8,128)(2,1)} copy(bf16[512,4096]{1,0:T(8,128)(2,1)} %convolution_convert_fusion) | data formatting | bytes 8388608 | tf_op jit(solution)/shard_map/convert_element_type | solution.py:135
  415.3 7.3 %copy.65 = bf16[512,4,2,512]{3,0,1,2:T(8,128)(2,1)} copy(bf16[512,4,2,512]{0,3,2,1:T(8,128)(2,1)} %bitcast.229) | data formatting | bytes 8388608 | tf_op jit(solution)/shard_map/reshape | solution.py:136
  422.6 3.8 select_bitcast_fusion
  426.4 4.5 collective-permute-done.33
  430.9 3.7 fusion.9
  434.9 2.7 collective-permute-start.35
  437.9 11.5 %collective-permute-done.34 = bf16[512,512]{1,0:T(8,128)(2,1)S(1)} collective-permute-done((bf16[512,512]{1,0:T(8,128)(2,1)S(1)}, bf16[512,512]{1,0:T(8,128)(2,1)S(1)}, u32[]{:S(2)}, u32[]{:S(2)}) %collective-permute-start.34) | collective-permute-done | bytes 524320 | tf_op jit(solution)/shard_map/ppermute | solution.py:12
  449.4 10.0 %collective-permute-done.35 = bf16[512,512]{1,0:T(8,128)(2,1)S(1)} collective-permute-done((bf16[512,512]{1,0:T(8,128)(2,1)S(1)}, bf16[512,512]{1,0:T(8,128)(2,1)S(1)}, u32[]{:S(2)}, u32[]{:S(2)}) %collective-permute-start.35) | collective-permute-done | bytes 524320 | tf_op jit(solution)/shard_map/ppermute | solution.py:12
  461.4 4.3 collective-permute-start.37
  465.7 7.7 %collective-permute-done.37 = bf16[512,512]{1,0:T(8,128)(2,1)S(1)} collective-permute-done((bf16[512,512]{1,0:T(8,128)(2,1)S(1)}, bf16[512,512]{1,0:T(8,128)(2,1)S(1)}, u32[]{:S(2)}, u32[]{:S(2)}) %collective-permute-start.37) | collective-permute-done | bytes 524320 | tf_op jit(solution)/shard_map/ppermute | solution.py:16
  (160 shorter events, 58.4 us)
Async XLA Ops:
  6.5 151.1 %all-gather.6.cloned.1.call-start = ((), (), s32[]{:S(2)}) async-start(), calls=%async_computation | async-start | bytes 13369344 | tf_op jit(solution)/shard_map/all_gather | solution.py:77
  9.2 16.3 %copy-start.4 = (bf16[512,512]{1,0:T(8,128)(2,1)S(1)}, bf16[512,512]{1,0:T(8,128)(2,1)}, u32[]{:S(2)}) copy-start(bf16[512,512]{1,0:T(8,128)(2,1)} %param.8) | copy-start | bytes 1572868
  9.2 16.4 %copy-start.6 = (bf16[2,512,256]{2,1,0:T(8,128)(2,1)S(1)}, bf16[2,512,256]{2,1,0:T(8,128)(2,1)}, u32[]{:S(2)}) copy-start(bf16[2,512,256]{2,1,0:T(8,128)(2,1)} %param.15) | copy-start | bytes 1572868
  9.2 290.6 %all-gather.8.cloned.1.call-start = ((), (), s32[]{:S(2)}) async-start(), calls=%async_computation.1 | async-start | bytes 13369344 | tf_op jit(solution)/shard_map/all_gather | solution.py:122
  9.5 21.5 %copy-start.10 = (f32[2,3,3,512]{3,0,2,1:T(2,128)S(1)}, f32[2,3,3,512]{3,0,2,1:T(2,128)}, u32[]{:S(2)}) copy-start(f32[2,3,3,512]{3,0,2,1:T(2,128)} %param.11) | copy-start | bytes 110596
  9.5 14.9 %collective-permute-start.29 = (bf16[256,1536]{0,1:T(8,128)(2,1)S(1)}, bf16[256,1536]{0,1:T(8,128)(2,1)S(1)}, u32[]{:S(2)}, u32[]{:S(2)}) collective-permute-start(bf16[256,1536]{0,1:T(8,128)(2,1)S(1)} %bitcast.245), channel_id=1, source_target_pairs={{1,8},{8,1},{3,10},{10,3},{5,12},{12,5},{7,14},{14,7},{17,24},{24,... | collective-permute-start | bytes 2359304 | tf_op jit(solution)/shard_map/ppermute | solution.py:16
  25.4 40.9 %copy-start.13 = (f32[2,512]{1,0:T(2,128)S(1)}, f32[2,512]{1,0:T(2,128)}, u32[]{:S(2)}) copy-start(f32[2,512]{1,0:T(2,128)} %param.14) | copy-start | bytes 12292
  25.4 41.1 %copy-start.12 = (f32[7,512]{1,0:T(8,128)S(1)}, f32[7,512]{1,0:T(8,128)}, u32[]{:S(2)}) copy-start(f32[7,512]{1,0:T(8,128)} %param.12) | copy-start | bytes 43012
  25.4 41.1 %copy-start.11 = (f32[2,4096]{1,0:T(2,128)S(1)}, f32[2,4096]{1,0:T(2,128)}, u32[]{:S(2)}) copy-start(f32[2,4096]{1,0:T(2,128)} %param.9) | copy-start | bytes 98308
  25.5 354.6 %all-gather.10.cloned.1.call-start = ((), (), s32[]{:S(2)}) async-start(), calls=%async_computation.2 | async-start | bytes 4456448 | tf_op jit(solution)/shard_map/all_gather | solution.py:124
  25.5 41.1 %collective-permute-start.1 = (bf16[512,512]{1,0:T(8,128)(2,1)S(1)}, bf16[512,512]{1,0:T(8,128)(2,1)S(1)}, u32[]{:S(2)}, u32[]{:S(2)}) collective-permute-start(bf16[512,512]{1,0:T(8,128)(2,1)S(1)} %copy-done.4), channel_id=1, source_target_pairs={{0,1},{1,0},{2,3},{3,2},{4,5},{5,4},{6,7},{7,6},{8,9},{9,8},{10,11... | collective-permute-start | bytes 1572872 | tf_op jit(solution)/shard_map/ppermute | solution.py:12
  25.8 14.4 %collective-permute-start.7 = (bf16[512,256]{0,1:T(8,128)(2,1)S(1)}, bf16[512,256]{0,1:T(8,128)(2,1)S(1)}, u32[]{:S(2)}, u32[]{:S(2)}) collective-permute-start(bf16[512,256]{0,1:T(8,128)(2,1)S(1)} %bitcast.250), channel_id=1, source_target_pairs={{0,64},{64,0},{1,65},{65,1},{2,66},{66,2},{3,67},{67,3},{4,68},{68... | collective-permute-start | bytes 786440 | tf_op jit(solution)/shard_map/ppermute | solution.py:12
  26.2 192.9 %collective-permute-start.32 = (bf16[512,256]{1,0:T(8,128)(2,1)S(1)}, bf16[512,256]{1,0:T(8,128)(2,1)}, u32[]{:S(2)}, u32[]{:S(2)}) collective-permute-start(bf16[512,256]{1,0:T(8,128)(2,1)S(1)} %get-tuple-element.44), channel_id=1, source_target_pairs={{1,8},{8,1},{3,10},{10,3},{5,12},{12,5},{7,14},{14,7},{17,24},{24,... | collective-permute-start | bytes 786440 | tf_op jit(solution)/shard_map/ppermute | solution.py:16
  40.5 38.5 %collective-permute-start.8 = (bf16[2,512,256]{1,2,0:T(8,128)(2,1)S(1)}, bf16[2,512,256]{1,2,0:T(8,128)(2,1)}, u32[]{:S(2)}, u32[]{:S(2)}) collective-permute-start(bf16[2,512,256]{1,2,0:T(8,128)(2,1)S(1)} %get-tuple-element.40), channel_id=1, source_target_pairs={{0,16},{16,32},{32,48},{48,0},{1,17},{17,33},{33,49},{49,1},{2,18}... | collective-permute-start | bytes 1572872 | tf_op jit(solution)/shard_map/ppermute | solution.py:12
  41.8 53.4 %collective-permute-start.9 = (bf16[2,512,256]{1,2,0:T(8,128)(2,1)S(1)}, bf16[2,512,256]{1,2,0:T(8,128)(2,1)}, u32[]{:S(2)}, u32[]{:S(2)}) collective-permute-start(bf16[2,512,256]{1,2,0:T(8,128)(2,1)S(1)} %get-tuple-element.40), channel_id=1, source_target_pairs={{0,32},{16,48},{32,0},{48,16},{1,33},{17,49},{33,1},{49,17},{2,34}... | collective-permute-start | bytes 1572872 | tf_op jit(solution)/shard_map/ppermute | solution.py:12
  66.3 34.0 %collective-permute-start.10 = (bf16[2,512,256]{1,2,0:T(8,128)(2,1)S(1)}, bf16[2,512,256]{1,2,0:T(8,128)(2,1)}, u32[]{:S(2)}, u32[]{:S(2)}) collective-permute-start(bf16[2,512,256]{1,2,0:T(8,128)(2,1)S(1)} %get-tuple-element.40), channel_id=1, source_target_pairs={{0,48},{16,0},{32,16},{48,32},{1,49},{17,1},{33,17},{49,33},{2,50}... | collective-permute-start | bytes 1572872 | tf_op jit(solution)/shard_map/ppermute | solution.py:12
  66.7 39.0 %collective-permute-start.11 = (bf16[2,512,256]{1,2,0:T(8,128)(2,1)S(1)}, bf16[2,512,256]{1,2,0:T(8,128)(2,1)S(1)}, u32[]{:S(2)}, u32[]{:S(2)}) collective-permute-start(bf16[2,512,256]{1,2,0:T(8,128)(2,1)S(1)} %get-tuple-element.40), channel_id=1, source_target_pairs={{0,8},{8,0},{1,9},{9,1},{2,10},{10,2},{3,11},{11,3},{4,12},{12,4},... | collective-permute-start | bytes 1572872 | tf_op jit(solution)/shard_map/ppermute | solution.py:12
  78.9 27.2 %collective-permute-start.12 = (bf16[2,512,256]{1,2,0:T(8,128)(2,1)}, bf16[2,512,256]{1,2,0:T(8,128)(2,1)S(1)}, u32[]{:S(2)}, u32[]{:S(2)}) collective-permute-start(bf16[2,512,256]{1,2,0:T(8,128)(2,1)} %collective-permute-done.8), channel_id=1, source_target_pairs={{0,8},{8,0},{1,9},{9,1},{2,10},{10,2},{3,11},{11,3},{4,12},{12,4},... | collective-permute-start | bytes 1572872 | tf_op jit(solution)/shard_map/ppermute | solution.py:12
  95.2 13.0 %collective-permute-start.13 = (bf16[2,512,256]{1,2,0:T(8,128)(2,1)}, bf16[2,512,256]{1,2,0:T(8,128)(2,1)S(1)}, u32[]{:S(2)}, u32[]{:S(2)}) collective-permute-start(bf16[2,512,256]{1,2,0:T(8,128)(2,1)} %collective-permute-done.9), channel_id=1, source_target_pairs={{0,8},{8,0},{1,9},{9,1},{2,10},{10,2},{3,11},{11,3},{4,12},{12,4},... | collective-permute-start | bytes 1572872 | tf_op jit(solution)/shard_map/ppermute | solution.py:12
  100.3 9.5 %collective-permute-start.14 = (bf16[2,512,256]{1,2,0:T(8,128)(2,1)}, bf16[2,512,256]{1,2,0:T(8,128)(2,1)S(1)}, u32[]{:S(2)}, u32[]{:S(2)}) collective-permute-start(bf16[2,512,256]{1,2,0:T(8,128)(2,1)} %collective-permute-done.10), channel_id=1, source_target_pairs={{0,8},{8,0},{1,9},{9,1},{2,10},{10,2},{3,11},{11,3},{4,12},{12,4},... | collective-permute-start | bytes 1572872 | tf_op jit(solution)/shard_map/ppermute | solution.py:12
  105.7 26.3 %collective-permute-start.2 = (bf16[512,1024]{1,0:T(8,128)(2,1)S(1)}, bf16[512,1024]{1,0:T(8,128)(2,1)S(1)}, u32[]{:S(2)}, u32[]{:S(2)}) collective-permute-start(bf16[512,1024]{1,0:T(8,128)(2,1)S(1)} %get-tuple-element.36), channel_id=1, source_target_pairs={{0,2},{2,4},{4,6},{6,0},{1,3},{3,5},{5,7},{7,1},{8,10},{10,12},{12... | collective-permute-start | bytes 3145736 | tf_op jit(solution)/shard_map/ppermute | solution.py:12
  106.1 47.9 %collective-permute-start.3 = (bf16[512,1024]{1,0:T(8,128)(2,1)S(1)}, bf16[512,1024]{1,0:T(8,128)(2,1)S(1)}, u32[]{:S(2)}, u32[]{:S(2)}) collective-permute-start(bf16[512,1024]{1,0:T(8,128)(2,1)S(1)} %get-tuple-element.36), channel_id=1, source_target_pairs={{0,4},{2,6},{4,0},{6,2},{1,5},{3,7},{5,1},{7,3},{8,12},{10,14},{12... | collective-permute-start | bytes 3145736 | tf_op jit(solution)/shard_map/ppermute | solution.py:12
  108.2 46.4 %collective-permute-start.4 = (bf16[512,1024]{1,0:T(8,128)(2,1)S(1)}, bf16[512,1024]{1,0:T(8,128)(2,1)S(1)}, u32[]{:S(2)}, u32[]{:S(2)}) collective-permute-start(bf16[512,1024]{1,0:T(8,128)(2,1)S(1)} %get-tuple-element.36), channel_id=1, source_target_pairs={{0,6},{2,0},{4,2},{6,4},{1,7},{3,1},{5,3},{7,5},{8,14},{10,8},{12,... | collective-permute-start | bytes 3145736 | tf_op jit(solution)/shard_map/ppermute | solution.py:12
  172.5 24.2 %collective-permute-start.5 = (bf16[2,512]{0,1:T(8,128)(2,1)S(1)}, bf16[2,512]{0,1:T(8,128)(2,1)S(1)}, u32[]{:S(2)}, u32[]{:S(2)}) collective-permute-start(bf16[2,512]{0,1:T(8,128)(2,1)S(1)} %slice_bitcast_fusion.10), channel_id=1, source_target_pairs={{0,8},{8,16},{16,24},{24,32},{32,40},{40,48},{48,56},{56,64},{64,7... | collective-permute-start | bytes 6152 | tf_op jit(solution)/shard_map/ppermute | solution.py:23
  192.7 12.4 %collective-permute-start.6 = (bf16[8,1024]{0,1:T(8,128)(2,1)S(1)}, bf16[8,1024]{0,1:T(8,128)(2,1)S(1)}, u32[]{:S(2)}, u32[]{:S(2)}) collective-permute-start(bf16[8,1024]{0,1:T(8,128)(2,1)S(1)} %bitcast.265), channel_id=1, source_target_pairs={{0,8},{8,16},{16,24},{24,32},{32,40},{40,48},{48,56},{56,64},{64,7... | collective-permute-start | bytes 49160 | tf_op jit(solution)/shard_map/ppermute | solution.py:23
  216.4 24.2 %collective-permute-start.15 = (bf16[512,1024]{1,0:T(8,128)(2,1)}, bf16[512,1024]{1,0:T(8,128)(2,1)S(1)}, u32[]{:S(2)}, u32[]{:S(2)}) collective-permute-start(bf16[512,1024]{1,0:T(8,128)(2,1)} %get-tuple-element.5), channel_id=1, source_target_pairs={{0,2},{2,4},{4,6},{6,0},{1,3},{3,5},{5,7},{7,1},{8,10},{10,12},{12... | collective-permute-start | bytes 3145736 | tf_op jit(solution)/shard_map/ppermute | solution.py:12
  216.4 25.6 %collective-permute-start.16 = (bf16[512,1024]{1,0:T(8,128)(2,1)}, bf16[512,1024]{1,0:T(8,128)(2,1)}, u32[]{:S(2)}, u32[]{:S(2)}) collective-permute-start(bf16[512,1024]{1,0:T(8,128)(2,1)} %get-tuple-element.7), channel_id=1, source_target_pairs={{0,6},{2,0},{4,2},{6,4},{1,7},{3,1},{5,3},{7,5},{8,14},{10,8},{12,... | collective-permute-start | bytes 3145736 | tf_op jit(solution)/shard_map/ppermute | solution.py:12
  219.1 39.1 %collective-permute-start.17 = (bf16[512,1024]{1,0:T(8,128)(2,1)S(1)}, bf16[512,1024]{1,0:T(8,128)(2,1)}, u32[]{:S(2)}, u32[]{:S(2)}) collective-permute-start(bf16[512,1024]{1,0:T(8,128)(2,1)S(1)} %get-tuple-element.6), channel_id=1, source_target_pairs={{0,4},{2,6},{4,0},{6,2},{1,5},{3,7},{5,1},{7,3},{8,12},{10,14},{12... | collective-permute-start | bytes 3145736 | tf_op jit(solution)/shard_map/ppermute | solution.py:12
  220.8 46.8 %collective-permute-start = (bf16[512,512]{1,0:T(8,128)(2,1)S(1)}, bf16[512,512]{1,0:T(8,128)(2,1)S(1)}, u32[]{:S(2)}, u32[]{:S(2)}) collective-permute-start(bf16[512,512]{1,0:T(8,128)(2,1)S(1)} %copy-done.5), channel_id=1, source_target_pairs={{1,8},{8,1},{3,10},{10,3},{5,12},{12,5},{7,14},{14,7},{17,24},{24,... | collective-permute-start | bytes 1572872 | tf_op jit(solution)/shard_map/ppermute | solution.py:16
  261.0 20.5 %copy-start.8 = (f32[128,512]{1,0:T(8,128)S(1)}, f32[128,512]{1,0:T(8,128)}, u32[]{:S(2)}) copy-start(f32[128,512]{1,0:T(8,128)} %param.13) | copy-start | bytes 786436
  261.1 9.5 %collective-permute-start.18 = (bf16[512,512]{1,0:T(8,128)(2,1)S(1)}, bf16[512,512]{1,0:T(8,128)(2,1)S(1)}, u32[]{:S(2)}, u32[]{:S(2)}) collective-permute-start(bf16[512,512]{1,0:T(8,128)(2,1)S(1)} %get-tuple-element.33), channel_id=1, source_target_pairs={{1,0},{8,9},{3,2},{10,11},{5,4},{12,13},{7,6},{14,15},{17,16},{24,... | collective-permute-start | bytes 1572872 | tf_op jit(solution)/shard_map/ppermute | solution.py:109
  264.5 13.2 %collective-permute-start.19 = (bf16[512,512]{1,0:T(8,128)(2,1)S(1)}, bf16[512,512]{1,0:T(8,128)(2,1)S(1)}, u32[]{:S(2)}, u32[]{:S(2)}) collective-permute-start(bf16[512,512]{1,0:T(8,128)(2,1)S(1)} %get-tuple-element.34), channel_id=1, source_target_pairs={{1,8},{8,1},{3,10},{10,3},{5,12},{12,5},{7,14},{14,7},{17,24},{24,... | collective-permute-start | bytes 1572872 | tf_op jit(solution)/shard_map/ppermute | solution.py:110
  266.4 11.3 %collective-permute-start.20 = (bf16[512,512]{1,0:T(8,128)(2,1)S(1)}, bf16[512,512]{1,0:T(8,128)(2,1)S(1)}, u32[]{:S(2)}, u32[]{:S(2)}) collective-permute-start(bf16[512,512]{1,0:T(8,128)(2,1)S(1)} %get-tuple-element.34), channel_id=1, source_target_pairs={{0,8},{9,1},{2,10},{11,3},{4,12},{13,5},{6,14},{15,7},{16,24},{25,... | collective-permute-start | bytes 1572872 | tf_op jit(solution)/shard_map/ppermute | solution.py:111
  278.1 19.8 %collective-permute-start.22 = (bf16[512,512]{1,0:T(8,128)(2,1)S(1)}, bf16[512,512]{1,0:T(8,128)(2,1)S(1)}, u32[]{:S(2)}, u32[]{:S(2)}) collective-permute-start(bf16[512,512]{1,0:T(8,128)(2,1)S(1)} %add_convert_fusion.1), channel_id=1, source_target_pairs={{0,2},{2,4},{4,6},{6,0},{1,3},{3,5},{5,7},{7,1},{8,10},{10,12},{12... | collective-permute-start | bytes 1572872 | tf_op jit(solution)/shard_map/ppermute | solution.py:12
  279.0 19.2 %collective-permute-start.23 = (bf16[512,512]{1,0:T(8,128)(2,1)S(1)}, bf16[512,512]{1,0:T(8,128)(2,1)S(1)}, u32[]{:S(2)}, u32[]{:S(2)}) collective-permute-start(bf16[512,512]{1,0:T(8,128)(2,1)S(1)} %add_convert_fusion.1), channel_id=1, source_target_pairs={{0,4},{2,6},{4,0},{6,2},{1,5},{3,7},{5,1},{7,3},{8,12},{10,14},{12... | collective-permute-start | bytes 1572872 | tf_op jit(solution)/shard_map/ppermute | solution.py:12
  280.2 18.4 %collective-permute-start.24 = (bf16[512,512]{1,0:T(8,128)(2,1)S(1)}, bf16[512,512]{1,0:T(8,128)(2,1)S(1)}, u32[]{:S(2)}, u32[]{:S(2)}) collective-permute-start(bf16[512,512]{1,0:T(8,128)(2,1)S(1)} %add_convert_fusion.1), channel_id=1, source_target_pairs={{0,6},{2,0},{4,2},{6,4},{1,7},{3,1},{5,3},{7,5},{8,14},{10,8},{12,... | collective-permute-start | bytes 1572872 | tf_op jit(solution)/shard_map/ppermute | solution.py:12
  281.5 17.2 %collective-permute-start.21 = (f32[138,512]{1,0:T(8,128)S(1)}, f32[138,512]{1,0:T(8,128)}, u32[]{:S(2)}, u32[]{:S(2)}) collective-permute-start(f32[138,512]{1,0:T(8,128)S(1)} %pad_maximum_fusion.11), channel_id=1, source_target_pairs={{1,8},{8,1},{3,10},{10,3},{5,12},{12,5},{7,14},{14,7},{17,24},{24,... | collective-permute-start | bytes 847880 | tf_op jit(solution)/shard_map/ppermute | solution.py:16
  288.0 40.9 %collective-permute-start.25 = (bf16[512,512]{1,0:T(8,128)(2,1)S(1)}, bf16[512,512]{1,0:T(8,128)(2,1)S(1)}, u32[]{:S(2)}, u32[]{:S(2)}) collective-permute-start(bf16[512,512]{1,0:T(8,128)(2,1)S(1)} %add_convert_fusion.1), channel_id=1, source_target_pairs={{0,8},{8,0},{1,9},{9,1},{2,10},{10,2},{3,11},{11,3},{4,12},{12,4},... | collective-permute-start | bytes 1572872 | tf_op jit(solution)/shard_map/ppermute | solution.py:12
  297.9 30.9 %collective-permute-start.26 = (bf16[512,512]{1,0:T(8,128)(2,1)S(1)}, bf16[512,512]{1,0:T(8,128)(2,1)}, u32[]{:S(2)}, u32[]{:S(2)}) collective-permute-start(bf16[512,512]{1,0:T(8,128)(2,1)S(1)} %collective-permute-done.22), channel_id=1, source_target_pairs={{0,8},{8,0},{1,9},{9,1},{2,10},{10,2},{3,11},{11,3},{4,12},{12,4},... | collective-permute-start | bytes 1572872 | tf_op jit(solution)/shard_map/ppermute | solution.py:12
  298.2 30.7 %collective-permute-start.27 = (bf16[512,512]{1,0:T(8,128)(2,1)S(1)}, bf16[512,512]{1,0:T(8,128)(2,1)}, u32[]{:S(2)}, u32[]{:S(2)}) collective-permute-start(bf16[512,512]{1,0:T(8,128)(2,1)S(1)} %collective-permute-done.23), channel_id=1, source_target_pairs={{0,8},{8,0},{1,9},{9,1},{2,10},{10,2},{3,11},{11,3},{4,12},{12,4},... | collective-permute-start | bytes 1572872 | tf_op jit(solution)/shard_map/ppermute | solution.py:12
  298.6 30.3 %collective-permute-start.28 = (bf16[512,512]{1,0:T(8,128)(2,1)S(1)}, bf16[512,512]{1,0:T(8,128)(2,1)}, u32[]{:S(2)}, u32[]{:S(2)}) collective-permute-start(bf16[512,512]{1,0:T(8,128)(2,1)S(1)} %collective-permute-done.24), channel_id=1, source_target_pairs={{0,8},{8,0},{1,9},{9,1},{2,10},{10,2},{3,11},{11,3},{4,12},{12,4},... | collective-permute-start | bytes 1572872 | tf_op jit(solution)/shard_map/ppermute | solution.py:12
  358.1 31.4 %collective-permute-start.31 = (bf16[129,1024]{1,0:T(8,128)(2,1)S(1)}, bf16[129,1024]{1,0:T(8,128)(2,1)}, u32[]{:S(2)}, u32[]{:S(2)}) collective-permute-start(bf16[129,1024]{1,0:T(8,128)(2,1)S(1)} %copy.58), channel_id=1, source_target_pairs={{0,1},{1,16},{16,17},{17,32},{32,33},{33,48},{48,49},{49,64},{64,6... | collective-permute-start | bytes 792584 | tf_op jit(solution)/shard_map/ppermute | solution.py:23
  363.1 26.1 %collective-permute-start.30 = (bf16[2,512]{1,0:T(2,128)(2,1)S(1)}, bf16[2,512]{1,0:T(2,128)(2,1)S(1)}, u32[]{:S(2)}, u32[]{:S(2)}) collective-permute-start(bf16[2,512]{1,0:T(2,128)(2,1)S(1)} %bitcast.270), channel_id=1, source_target_pairs={{0,1},{1,16},{16,17},{17,32},{32,33},{33,48},{48,49},{49,64},{64,6... | collective-permute-start | bytes 6152 | tf_op jit(solution)/shard_map/ppermute | solution.py:23
  426.4 4.5 collective-permute-start.33
  434.8 14.7 %collective-permute-start.34 = (bf16[512,512]{1,0:T(8,128)(2,1)S(1)}, bf16[512,512]{1,0:T(8,128)(2,1)S(1)}, u32[]{:S(2)}, u32[]{:S(2)}) collective-permute-start(bf16[512,512]{1,0:T(8,128)(2,1)S(1)} %get-tuple-element.12), channel_id=1, source_target_pairs={{0,2},{2,4},{4,6},{6,0},{1,3},{3,5},{5,7},{7,1},{8,10},{10,12},{12... | collective-permute-start | bytes 1572872 | tf_op jit(solution)/shard_map/ppermute | solution.py:12
  434.9 24.6 %collective-permute-start.35 = (bf16[512,512]{1,0:T(8,128)(2,1)S(1)}, bf16[512,512]{1,0:T(8,128)(2,1)S(1)}, u32[]{:S(2)}, u32[]{:S(2)}) collective-permute-start(bf16[512,512]{1,0:T(8,128)(2,1)S(1)} %get-tuple-element.14), channel_id=1, source_target_pairs={{0,6},{2,0},{4,2},{6,4},{1,7},{3,1},{5,3},{7,5},{8,14},{10,8},{12,... | collective-permute-start | bytes 1572872 | tf_op jit(solution)/shard_map/ppermute | solution.py:12
  437.5 23.5 %collective-permute-start.36 = (bf16[512,512]{1,0:T(8,128)(2,1)S(1)}, bf16[512,512]{1,0:T(8,128)(2,1)S(1)}, u32[]{:S(2)}, u32[]{:S(2)}) collective-permute-start(bf16[512,512]{1,0:T(8,128)(2,1)S(1)} %get-tuple-element.13), channel_id=1, source_target_pairs={{0,4},{2,6},{4,0},{6,2},{1,5},{3,7},{5,1},{7,3},{8,12},{10,14},{12... | collective-permute-start | bytes 1572872 | tf_op jit(solution)/shard_map/ppermute | solution.py:12
  461.4 12.0 %collective-permute-start.37 = (bf16[512,512]{1,0:T(8,128)(2,1)S(1)}, bf16[512,512]{1,0:T(8,128)(2,1)S(1)}, u32[]{:S(2)}, u32[]{:S(2)}) collective-permute-start(bf16[512,512]{1,0:T(8,128)(2,1)S(1)} %fusion.47), channel_id=1, source_target_pairs={{1,8},{8,1},{3,10},{10,3},{5,12},{12,5},{7,14},{14,7},{17,24},{24,... | collective-permute-start | bytes 1572872 | tf_op jit(solution)/shard_map/ppermute | solution.py:16
  (7 other events, 30.5 us)
Sparse Core Ops, SparseCore 0:
  9.3 118.3 all-gather.5
  129.9 105.1 all-gather.7
  237.2 59.7 all-gather.9

commit v2 on v1

v2 whole, which is shorter than its diff:
```python
import functools

import jax
import jax.numpy as jnp
import numpy as np
from jax import lax
from jax.experimental import pallas as pl
from jax.experimental.pallas import tpu as pltpu
from jax.sharding import Mesh, PartitionSpec as P

AXES = ("xl", "y", "core", "z", "xh")
ROWS = 512
LANES = 128


def shift(value, axis, by):
    size = lax.axis_size(axis)
    return lax.ppermute(value, axis, [(i, (i + by) % size) for i in range(size)])


def shift_x(value, by):
    place = lambda x: (x % 2) * 2 + x // 2
    return lax.ppermute(value, ("xl", "xh"), [(place(x), place((x + by) % 4)) for x in range(4)])


def shift_y(value, by):
    return shift(value, "y", by)


def swap(value):
    moved = lax.ppermute(value, ("core", "xh"), [(1, 2), (2, 1)])
    same = lax.axis_index("core") == lax.axis_index("xh")
    return jnp.where(same, value, moved)


def from_behind(value, axes):
    return lax.ppermute(value, axes, [(i, i + 1) for i in range(15)])


def after(value, *others):
    return lax.optimization_barrier((value, *others))[0]


def ring_four(value, move):
    one = move(value, 1)
    three = move(value, -1)
    low = move(one[:2], 1)
    high = move(three[2:], -1)
    return one, three, low, high


def fetch(moves, sources, target, index_ref, semaphores):
    copies = []
    for number, (source, lead, lane, width, slot, other, by_rows) in enumerate(moves):
        block = pl.multiple_of(index_ref[slot] * 256, 256)
        ref = sources[source]
        if lead is not None:
            ref = ref.at[lead]
        if by_rows:
            piece = target.at[pl.ds(block, 256), other : other + width]
        else:
            piece = target.at[other : other + ref.shape[0], pl.ds(block, 256)]
        copies.append(pltpu.make_async_copy(ref.at[:, lane : lane + width], piece, semaphores.at[number]))
    return copies


def in_kernel(moves, pieces, halo, index_ref, gain_ref, *refs):
    xs, refs = refs[:pieces], refs[pieces:]
    count = 1 + max(m[0] for m in moves)
    ws, refs = refs[:count], refs[count:]
    out_ref, tail_ref, raw, normed, weights, squares, x_sems, w_sems = refs
    loads = [pltpu.make_async_copy(x, raw.at[j], x_sems.at[j]) for j, x in enumerate(xs)]
    for load in loads:
        load.start()
    copies = fetch(moves, ws, weights, index_ref, w_sems)
    for copy in copies:
        copy.start()
    squares[...] = jnp.zeros_like(squares)
    for j, load in enumerate(loads):
        load.wait()
        block = index_ref[j]
        lanes = pl.ds(pl.multiple_of(block * 512, 512), 512)
        gain = gain_ref[pl.ds(block, 1), :]

        @pl.loop(0, ROWS // 64)
        def _(step):
            rows = pl.ds(pl.multiple_of(step * 64, 64), 64)
            x = raw[j, rows, :].astype(jnp.float32)
            normed[rows, lanes] = (x * gain).astype(jnp.bfloat16)
            q = x * x
            squares[rows, :] += (q[:, :128] + q[:, 128:256]) + (q[:, 256:384] + q[:, 384:])

    squares[:, :1] = lax.rsqrt(jnp.sum(squares[...], axis=1, keepdims=True) * (1.0 / 4096) + 1e-06)
    for copy in copies:
        copy.wait()

    @pl.loop(0, 6)
    def _(step):
        lanes = pl.ds(pl.multiple_of(step * 256, 256), 256)
        product = jnp.dot(normed[...], weights[:, lanes], preferred_element_type=jnp.float32)
        out_ref[:, lanes] = (product * squares[:, :1]).astype(jnp.bfloat16)

    tail_ref[:halo, :] = out_ref[ROWS - halo :, 512:]
    tail_ref[halo:, :512] = out_ref[ROWS - 16 :, :512]
    tail_ref[halo:, 512:] = jnp.zeros((16, 512), jnp.bfloat16)


def project_in(index, gain, pieces, weights, moves, halo):
    any_space = pl.BlockSpec(memory_space=pl.ANY)
    vmem = pl.BlockSpec(memory_space=pltpu.VMEM)
    return pl.pallas_call(
        functools.partial(in_kernel, moves, len(pieces), halo),
        out_shape=[
            jax.ShapeDtypeStruct((ROWS, 1536), jnp.bfloat16),
            jax.ShapeDtypeStruct((halo + 16, 1024), jnp.bfloat16),
        ],
        in_specs=[pl.BlockSpec(memory_space=pltpu.SMEM), vmem] + [any_space] * (len(pieces) + len(weights)),
        out_specs=[vmem, vmem],
        scratch_shapes=[
            pltpu.VMEM((len(pieces), ROWS, 512), jnp.bfloat16),
            pltpu.VMEM((ROWS, 4096), jnp.bfloat16),
            pltpu.VMEM((4096, 1536), jnp.bfloat16),
            pltpu.VMEM((ROWS, LANES), jnp.float32),
            pltpu.SemaphoreType.DMA((len(pieces),)),
            pltpu.SemaphoreType.DMA((len(moves),)),
        ],
        compiler_params=pltpu.CompilerParams(vmem_limit_bytes=44 * 1024 * 1024),
        cost_estimate=pl.CostEstimate(flops=2 * ROWS * 4096 * 1536, bytes_accessed=18 * 2**20, transcendentals=0),
    )(index, gain, *pieces, *weights)


def mix_kernel(moves, halo, taps, outs, index_ref, tail_ref, main_ref, feat_ref, filter_ref, skip_ref, *refs):
    count = 1 + max(m[0] for m in moves)
    ws, refs = refs[:count], refs[count:]
    out_refs, refs = refs[:outs], refs[outs:]
    shaped, gated, copies8, inner, weights, w_sems = refs
    copies = fetch(moves, ws, weights, index_ref, w_sems)
    for copy in copies:
        copy.start()
    total = halo + ROWS

    shaped[:16, :512] = tail_ref[halo:, :512].astype(jnp.float32)
    shaped[16 : 16 + ROWS, :512] = main_ref[:, :512].astype(jnp.float32)
    shaped[:halo, 512:] = tail_ref[:halo, :].astype(jnp.float32)
    shaped[halo:total, 512:] = main_ref[:, 512:].astype(jnp.float32)

    def feature(start, size, s, lanes):
        value = None
        for j in range(3):
            tap = feat_ref[3 * j + s : 3 * j + s + 1, lanes]
            low = s * 512 + lanes.start
            term = tap * shaped[start - j : start - j + size, low : low + LANES]
            value = term if value is None else value + term
        return value

    for lane in range(0, 512, LANES):
        lanes = slice(lane, lane + LANES)
        for start in range(8, total, 64):
            size = min(64, total - start)
            gated[start : start + size, lanes] = feature(start, size, 1, lanes) * feature(start, size, 2, lanes)
        gated[:8, lanes] = jnp.zeros((8, LANES), jnp.float32)

    if taps == 7:
        for lane in range(0, 512, LANES):
            lanes = slice(lane, lane + LANES)
            for start in range(0, ROWS, 64):
                own = gated[halo + start : halo + start + 64, lanes]
                value = (skip_ref[:1, lanes] + filter_ref[:1, lanes]) * own
                for j in range(1, taps):
                    value = value + filter_ref[j : j + 1, lanes] * gated[halo + start - j : halo + start - j + 64, lanes]
                inner[start : start + 64, lanes] = (feature(16 + start, 64, 0, lanes) * value).astype(jnp.bfloat16)
    else:
        for lane in range(0, 512, LANES):
            lanes = slice(lane, lane + LANES)
            for r in range(8):
                for start in range(0, ROWS + 128, 128):
                    copies8[r, start : start + 128, :] = gated[16 + start - r : 16 + start - r + 128, lanes]

            @pl.loop(0, ROWS // 128)
            def _(step):
                base = pl.multiple_of(step * 128, 128)
                value = jnp.zeros((128, LANES), jnp.float32)
                for r in range(8):
                    for a in range(0, 16, 4):
                        window = copies8[r, pl.ds(pl.multiple_of(base + 128 - 8 * (a + 3), 8), 128 + 24), :]
                        for b in range(4):
                            tap = filter_ref[8 * (a + b) + r : 8 * (a + b) + r + 1, lanes]
                            low = 8 * (3 - b)
                            value = value + tap * window[low : low + 128]
                copies8[8, pl.ds(base, 128), :] = value

            for start in range(0, ROWS, 64):
                own = gated[halo + start : halo + start + 64, lanes]
                value = copies8[8, start : start + 64, :] + skip_ref[:1, lanes] * own
                inner[start : start + 64, lanes] = (feature(16 + start, 64, 0, lanes) * value).astype(jnp.bfloat16)

    for copy in copies:
        copy.wait()
    z = index_ref[16]
    core = index_ref[17]
    for by in range(4):
        block = lax.rem(z + by, 4)
        if outs == 4:
            columns = pl.ds(pl.multiple_of(block * 1024, 1024), 1024)
            out_refs[by][...] = jnp.dot(
                inner[...], weights[:, columns], preferred_element_type=jnp.float32
            ).astype(jnp.bfloat16)
        else:
            for side in range(2):
                place = block * 2 + (core if side == 0 else 1 - core)
                columns = pl.ds(pl.multiple_of(place * 512, 512), 512)
                out_refs[side][by] = jnp.dot(
                    inner[...], weights[:, columns], preferred_element_type=jnp.float32
                ).astype(jnp.bfloat16)


def mix_out(index, tail, main, feat, taps, skip, weights, moves, halo, out_shapes):
    any_space = pl.BlockSpec(memory_space=pl.ANY)
    vmem = pl.BlockSpec(memory_space=pltpu.VMEM)
    length = taps.shape[0]
    small = length == 7
    return pl.pallas_call(
        functools.partial(mix_kernel, moves, halo, length, len(out_shapes)),
        out_shape=[jax.ShapeDtypeStruct(s, jnp.bfloat16) for s in out_shapes],
        in_specs=[pl.BlockSpec(memory_space=pltpu.SMEM)] + [vmem] * 5 + [any_space] * len(weights),
        out_specs=[vmem] * len(out_shapes),
        scratch_shapes=[
            pltpu.VMEM((halo + ROWS + 16, 1536), jnp.float32),
            pltpu.VMEM((halo + ROWS, 512), jnp.float32),
            pltpu.VMEM((9, 8, LANES) if small else (9, ROWS + 128, LANES), jnp.float32),
            pltpu.VMEM((ROWS, 512), jnp.bfloat16),
            pltpu.VMEM((512, 4096), jnp.bfloat16),
            pltpu.SemaphoreType.DMA((len(moves),)),
        ],
        compiler_params=pltpu.CompilerParams(vmem_limit_bytes=44 * 1024 * 1024),
        cost_estimate=pl.CostEstimate(
            flops=2 * ROWS * 512 * 4096 * (1 if small else 4), bytes_accessed=10 * 2**20, transcendentals=0
        ),
    )(index, tail, main, feat, taps, skip, *weights)


def per_device(hidden, norm_gain, in_weight, feat_filter, se_filter, mr_filter, skip_gain, out_weight):
    xl, y, core, z, xh = (lax.axis_index(a) for a in AXES)
    x = 2 * xh + xl
    behind = lambda place, by: (place - by) % 4
    gains = norm_gain.reshape(2, 8, 512)

    partner = shift(hidden, "xh", 1)
    x_pieces, x_slots = [hidden], [z * 2 + xh]
    for by in (1, -1, 2):
        x_pieces.append(shift(hidden, "z", by))
        x_slots.append(behind(z, by) * 2 + xh)
    w = in_weight[0].reshape(256, 1536)
    w_xl = shift(w, "xl", 1)
    w_y = {by: shift_y(w, by) for by in (1, -1, 2)}
    x_pieces.append(partner)
    x_slots.append(z * 2 + 1 - xh)
    for by in (1, -1, 2):
        x_pieces.append(shift(partner, "z", by))
        x_slots.append(behind(z, by) * 2 + 1 - xh)

    held = [(w, xl, y, 0, 1536), (w_xl, 1 - xl, y, 0, 1536)]
    held += [(w_y[by], xl, behind(y, by), 0, 1536) for by in (1, -1, 2)]
    held += [(shift_y(w_xl[:, :768], by), 1 - xl, behind(y, by), 0, 768) for by in (1, -1, 2)]
    held += [(shift(w_y[by][:, 768:], "xl", 1), 1 - xl, behind(y, by), 768, 768) for by in (1, -1, 2)]
    w_list, w_moves, w_slots = [], [], []
    for c, get in ((core, lambda v: v), (1 - core, lambda v: shift(v, "core", 1))):
        for value, at_xl, at_y, lane, width in held:
            w_moves.append((len(w_list), None, 0, width, 8 + len(w_slots), lane, True))
            w_list.append(get(value))
            w_slots.append(at_xl * 8 + at_y * 2 + c)
    index = jnp.stack(x_slots + w_slots).astype(jnp.int32)
    projected, tail = project_in(index, gains[0], x_pieces, w_list, w_moves, 16)

    o = after(out_weight[0], w_list[8], w_list[10])
    o_duo = jnp.stack([o, shift(o, "xl", 1)])
    o_held = [o_duo] + [shift_y(o_duo, by) for by in (1, -1, 2)]
    o_list, o_moves, o_slots = [], [], []
    for c, get in ((core, lambda v: v), (1 - core, lambda v: shift(v, "core", 1))):
        for value, by in zip(o_held, (0, 1, -1, 2)):
            for e in range(2):
                o_moves.append((len(o_list), e, 0, 256, len(o_slots), 0, False))
                o_slots.append((xl if e == 0 else 1 - xl) * 8 + behind(y, by) * 2 + c)
            o_list.append(get(value))
    o_index = jnp.stack(o_slots + [z, core]).astype(jnp.int32)

    small = swap(jnp.concatenate([feat_filter[1].reshape(9, 512), skip_gain[1:2], mr_filter], axis=0))
    m = jnp.concatenate(
        [in_weight[1].reshape(256, 1536), out_weight[1, :256], out_weight[1, 256:]], axis=1
    )
    m = after(swap(m), w_list[8], w_list[10])
    a, b = m[:, :1024], m[:, 1024:]
    a4 = jnp.stack([a] + [shift_x(a, by) for by in (1, -1, 2)])
    b4 = jnp.stack([b] + [shift_y(b, by) for by in (1, -1, 2)])
    a_lists = (a4,) + ring_four(a4, shift_y)
    b_lists = (b4,) + ring_four(b4, shift_x)
    hops = (0, 1, -1, 2)
    block_of = lambda at_x, at_y: (at_x % 2) * 8 + at_y * 2 + at_x // 2
    w_list, w_moves, w_slots = [], [], []
    q_list, q_moves, q_slots = [], [], []
    for is_b, lists in ((False, a_lists), (True, b_lists)):
        for value, by, entries in zip(lists, (0, 1, -1, 2, 2), (range(4), range(4), range(4), (0, 1), (2, 3))):
            for lead, e in enumerate(entries):
                near, far = (y, x) if is_b else (x, y)
                near, far = behind(near, hops[e]), behind(far, by)
                slot = block_of(far, near) if is_b else block_of(near, far)
                if is_b:
                    w_moves.append((len(w_list), lead, 0, 512, 8 + len(w_slots), 1024, True))
                    for half in range(2):
                        q_moves.append((len(q_list), lead, 512 + 256 * half, 256, len(q_slots), 256 * half, False))
                    q_slots.append(slot)
                else:
                    w_moves.append((len(w_list), lead, 0, 1024, 8 + len(w_slots), 0, True))
                w_slots.append(slot)
            w_list.append(value)
            if is_b:
                q_list.append(value)

    tail = from_behind(tail, ("xl", "y", "core"))
    parts = mix_out(
        o_index, tail, projected, feat_filter[0].reshape(9, 512), se_filter, skip_gain[0:1], o_list, o_moves, 16,
        [(ROWS, 1024)] * 4,
    )
    total = parts[0].astype(jnp.float32)
    for by, part in ((1, parts[1]), (-1, parts[3]), (2, parts[2])):
        total = total + shift(part, "z", by).astype(jnp.float32)
    total = total.astype(jnp.bfloat16)
    pick = lambda c: jnp.where(c == 0, total[:, :512], total[:, 512:])
    mine, others = pick(core), pick(1 - core)
    first = lax.ppermute(mine, ("core", "xh"), [(1, 0), (2, 3)])
    second = lax.ppermute(others, ("core", "xh"), [(1, 2), (2, 1)])
    third = lax.ppermute(others, ("core", "xh"), [(0, 2), (3, 1)])
    kept = jnp.where(core == xh, mine, jnp.zeros_like(mine))
    current = swap(hidden).astype(jnp.float32) + kept.astype(jnp.float32)
    for value in (first, second, third):
        current = current + value.astype(jnp.float32)
    current = current.astype(jnp.bfloat16)

    x_pieces, x_slots = [], []
    near = [current] + [shift(current, "z", by) for by in (1, -1, 2)]
    for side, values in ((core, near), (1 - core, [shift(v, "core", 1) for v in near])):
        for value, by in zip(values, hops):
            x_pieces.append(value)
            x_slots.append(behind(z, by) * 2 + side)
    index = jnp.stack(x_slots + w_slots).astype(jnp.int32)
    projected, tail = project_in(index, gains[1], x_pieces, w_list, w_moves, 144)
    tail = from_behind(tail, ("xl", "y", "xh"))
    q_slots = q_slots + [z, core]
    own, theirs = mix_out(
        jnp.stack(q_slots).astype(jnp.int32), tail, projected, small[:9], small[10:], small[9:10], q_list, q_moves, 144,
        [(4, ROWS, 512)] * 2,
    )
    both = (own.astype(jnp.float32) + shift(theirs, "core", 1).astype(jnp.float32)).astype(jnp.bfloat16)
    total = current.astype(jnp.float32) + both[0].astype(jnp.float32)
    for by, place in ((1, 1), (-1, 3), (2, 2)):
        total = total + shift(both[place], "z", by).astype(jnp.float32)
    return swap(total.astype(jnp.bfloat16))


def solution(mesh):
    fine = Mesh(np.asarray(mesh.devices).reshape(2, 4, 2, 4, 2), AXES)
    ctx, ch = ("xl", "y", "core"), ("z", "xh")
    return jax.shard_map(
        per_device,
        mesh=fine,
        in_specs=(
            P(ctx, ch),
            P(),
            P(None, ctx, None, ch),
            P(None, None, None, ch),
            P(None, ch),
            P(None, ch),
            P(None, ch),
            P(None, ch, ctx),
        ),
        out_specs=P(ctx, ch),
        check_vma=False,
    )
```

time: 488 us -> 489 us (level)
  the two profiles are of different devices: /device:TPU:11 before, /device:TPU:41 now
where the time goes in v2:
time: 489 us; the launch traced here: 480 us
  waiting for transfers between devices  258 us (53%)
  starting transfers between devices  112 us (23%)
  Pallas kernels  51 us (10%)
  local copies, waits for them, and re-layouts  42.1 us (9%)
  other arithmetic  14.8 us (3%)
    ppermute x57, waiting for transfers between devices, shift(): lax.ppermute(value, axis, [(i, (i + by) % size) for i in range(size)])  168 us
    ppermute x57, starting transfers between devices, shift(): lax.ppermute(value, axis, [(i, (i + by) % size) for i in range(size)])  70.5 us
    ppermute x4, waiting for transfers between devices, swap(): moved = lax.ppermute(value, ('core', 'xh'), [(1, 2), (2, 1)])  52.1 us
    pallas_call x2, Pallas kernels, project_in(): pl.pallas_call(functools.partial(in_kernel, moves, len(pieces), halo), ou...  26.5 us
    pallas_call x2, Pallas kernels, mix_out(): pl.pallas_call(functools.partial(mix_kernel, moves, halo, length, len(out...  24.4 us
    unnamed x94, local copies, waits for them, and re-layouts  21.5 us
    ppermute x7, waiting for transfers between devices, shift_x(): lax.ppermute(value, ('xl', 'xh'), [(place(x), place((x + by) % 4)) for x...  19.6 us
    ppermute x7, starting transfers between devices, shift_x(): lax.ppermute(value, ('xl', 'xh'), [(place(x), place((x + by) % 4)) for x...  16.9 us
  transfers between devices with their start and end apart: 73, of which 26 were waited for; matrix products, arithmetic and copies ran while one was open for 8% of the time, Pallas kernels for 7%

profile of v2, /device:TPU:41, one launch (start us, length us, event | category | flops | bytes accessed | tf_op | source)
XLA Modules:
  0.0 479.9 jit_solution(13034012752611753153)
XLA Ops:
  1.6 2.5 collective-permute-start.3
  4.2 2.4 fusion.4
  10.4 2.5 collective-permute-start.4
  14.6 12.0 %collective-permute-done.3.refs_3_ = bf16[512,512]{1,0:T(8,128)(2,1)S(1)} collective-permute-done((bf16[512,512]{1,0:T(8,128)(2,1)}, bf16[512,512]{1,0:T(8,128)(2,1)S(1)}, u32[]{:S(2)}, u32[]{:S(2)}) %collective-permute-start.3) | collective-permute-done | bytes 524320 | tf_op jit(solution)/shard_map/ppermute | solution.py:18
  29.6 2.3 copy.23
  32.0 2.3 copy.19
  34.3 6.0 %collective-permute-done.4.refs_4_ = bf16[512,512]{1,0:T(8,128)(2,1)} collective-permute-done((bf16[512,512]{1,0:T(8,128)(2,1)S(1)}, bf16[512,512]{1,0:T(8,128)(2,1)}, u32[]{:S(2)}, u32[]{:S(2)}) %collective-permute-start.4) | collective-permute-done | bytes 524320 | tf_op jit(solution)/shard_map/ppermute | solution.py:18
  40.3 2.4 collective-permute-start.18
  44.1 2.3 collective-permute-start.51
  51.6 9.1 %collective-permute-done.5.refs_5_ = bf16[512,512]{1,0:T(8,128)(2,1)S(1)} collective-permute-done((bf16[512,512]{1,0:T(8,128)(2,1)}, bf16[512,512]{1,0:T(8,128)(2,1)S(1)}, u32[]{:S(2)}, u32[]{:S(2)}) %collective-permute-start.5) | collective-permute-done | bytes 524320 | tf_op jit(solution)/shard_map/ppermute | solution.py:18
  64.5 8.3 %collective-permute-done.7.refs_7_ = bf16[512,512]{1,0:T(8,128)(2,1)S(1)} collective-permute-done((bf16[512,512]{1,0:T(8,128)(2,1)}, bf16[512,512]{1,0:T(8,128)(2,1)S(1)}, u32[]{:S(2)}, u32[]{:S(2)}) %collective-permute-start.7) | collective-permute-done | bytes 524320 | tf_op jit(solution)/shard_map/ppermute | solution.py:18
  77.9 5.1 %collective-permute-done.15.refs_16_ = bf16[256,768]{1,0:T(8,128)(2,1)S(1)} collective-permute-done((bf16[256,768]{1,0:T(8,128)(2,1)S(1)}, bf16[256,768]{1,0:T(8,128)(2,1)S(1)}, u32[]{:S(2)}, u32[]{:S(2)}) %collective-permute-start.15) | collective-permute-done | bytes 393248 | tf_op jit(solution)/shard_map/ppermute | solution.py:18
  83.0 2.3 collective-permute-start.21
  85.3 6.1 %collective-permute-done.17.refs_18_ = bf16[256,768]{1,0:T(8,128)(2,1)S(1)} collective-permute-done((bf16[256,768]{1,0:T(8,128)(2,1)S(1)}, bf16[256,768]{1,0:T(8,128)(2,1)S(1)}, u32[]{:S(2)}, u32[]{:S(2)}) %collective-permute-start.17) | collective-permute-done | bytes 393248 | tf_op jit(solution)/shard_map/ppermute | solution.py:18
  91.5 2.3 collective-permute-start.22
  93.8 6.1 %collective-permute-done.16.refs_17_ = bf16[256,768]{1,0:T(8,128)(2,1)S(1)} collective-permute-done((bf16[256,768]{1,0:T(8,128)(2,1)S(1)}, bf16[256,768]{1,0:T(8,128)(2,1)S(1)}, u32[]{:S(2)}, u32[]{:S(2)}) %collective-permute-start.16) | collective-permute-done | bytes 393248 | tf_op jit(solution)/shard_map/ppermute | solution.py:18
  99.9 6.4 %collective-permute-done.30 = bf16[512,256]{1,0:T(8,128)(2,1)S(1)} collective-permute-done((bf16[512,256]{1,0:T(8,128)(2,1)S(1)}, bf16[512,256]{1,0:T(8,128)(2,1)S(1)}, u32[]{:S(2)}, u32[]{:S(2)}) %collective-permute-start.30) | collective-permute-done | bytes 262176 | tf_op jit(solution)/shard_map/ppermute | solution.py:18
  106.3 2.3 collective-permute-start.23
  115.1 7.7 %collective-permute-done.31.refs_1_ = bf16[2,512,256]{2,1,0:T(8,128)(2,1)} collective-permute-done((bf16[2,512,256]{2,1,0:T(8,128)(2,1)S(1)}, bf16[2,512,256]{2,1,0:T(8,128)(2,1)}, u32[]{:S(2)}, u32[]{:S(2)}) %collective-permute-start.31) | collective-permute-done | bytes 524320 | tf_op jit(solution)/shard_map/ppermute | solution.py:18
  124.2 10.0 %collective-permute-done.32.refs_2_ = bf16[2,512,256]{2,1,0:T(8,128)(2,1)} collective-permute-done((bf16[2,512,256]{2,1,0:T(8,128)(2,1)S(1)}, bf16[2,512,256]{2,1,0:T(8,128)(2,1)}, u32[]{:S(2)}, u32[]{:S(2)}) %collective-permute-start.32) | collective-permute-done | bytes 524320 | tf_op jit(solution)/shard_map/ppermute | solution.py:18
  136.2 13.5 %shard_map.82 = (bf16[512,1536]{1,0:T(8,128)(2,1)}, bf16[32,1024]{1,0:T(8,128)(2,1)S(1)}) custom-call(s32[30]{0:T(128)S(1)} %stack.296.index_ref, f32[8,512]{1,0:T(8,128)S(1)} %squeeze.25.gain_ref, bf16[512,512]{1,0:T(8,128)(2,1)S(1)} %copy-done, bf16[512,512]{1,0:T(8,128)(2,1)S(1)} %collective-permute-done.1.refs_1_, ...), custom_call_target="tpu_custom_call" | custom-call | flops 6442450944 | bytes 18874368 | tf_op jit(solution)/shard_map/pallas_call | solution.py:111
  154.7 2.4 collective-permute-start.53
  165.4 5.6 %shard_map.83 = (bf16[512,1024]{1,0:T(8,128)(2,1)S(1)}, bf16[512,1024]{1,0:T(8,128)(2,1)S(1)}, bf16[512,1024]{1,0:T(8,128)(2,1)S(1)}, bf16[512,1024]{1,0:T(8,128)(2,1)S(1)}) custom-call(s32[18]{0:T(128)S(1)} %stack.283.index_ref, bf16[32,1024]{1,0:T(8,128)(2,1)S(1)} %collective-permute-done.29.tail_ref, bf16[512,1536]{1,0:T(8,128)(2,1)S(1)} %copy-done.28, ...), custom_call_target="tpu_custom_call" | custom-call | flops 2147483648 | bytes 10485760 | tf_op jit(solution)/shard_map/pallas_call | solution.py:222
  171.0 8.7 %collective-permute-start.40 = (bf16[512,1024]{1,0:T(8,128)(2,1)S(1)}, bf16[512,1024]{1,0:T(8,128)(2,1)S(1)}, u32[]{:S(2)}, u32[]{:S(2)}) collective-permute-start(bf16[512,1024]{1,0:T(8,128)(2,1)S(1)} %get-tuple-element.23), channel_id=1, source_target_pairs={{0,4},{2,6},{4,0},{6,2},{1,5},{3,7},{5,1},{7,3},{8,12},{10,14},{12... | collective-permute-start | bytes 3145736 | tf_op jit(solution)/shard_map/ppermute | solution.py:18
  179.7 3.3 collective-permute-start.39
  183.0 3.1 pad_maximum_fusion.refs_8_
  186.1 3.8 collective-permute-start.55
  190.2 54.9 %collective-permute-done.59 = bf16[256,1024]{1,0:T(8,128)(2,1)S(1)} collective-permute-done((bf16[256,1024]{1,0:T(8,128)(2,1)}, bf16[256,1024]{1,0:T(8,128)(2,1)S(1)}, u32[]{:S(2)}, u32[]{:S(2)}) %collective-permute-start.59) | collective-permute-done | bytes 524320 | tf_op jit(solution)/shard_map/ppermute | solution.py:18
  247.7 5.1 %collective-permute-start.62 = (bf16[4,256,1024]{2,1,0:T(8,128)(2,1)}, bf16[4,256,1024]{2,1,0:T(8,128)(2,1)}, u32[]{:S(2)}, u32[]{:S(2)}) collective-permute-start(bf16[4,256,1024]{2,1,0:T(8,128)(2,1)} %pad_maximum_fusion.1.refs_13_.refs_0_), channel_id=1, source_target_pairs={{0,64},{64,1},{1,65},{65,0},{2,66},{66,3},{3,67},{67,2},{4,68},{68... | collective-permute-start | bytes 6291464 | tf_op jit(solution)/shard_map/ppermute | solution.py:23
  254.2 6.0 %collective-permute-start = (bf16[512,512]{1,0:T(8,128)(2,1)S(1)}, bf16[512,512]{1,0:T(8,128)(2,1)S(1)}, u32[]{:S(2)}, u32[]{:S(2)}) collective-permute-start(bf16[512,512]{1,0:T(8,128)(2,1)S(1)} %copy-done), channel_id=1, source_target_pairs={{1,8},{8,1},{3,10},{10,3},{5,12},{12,5},{7,14},{14,7},{17,24},{24,... | collective-permute-start | bytes 1572872 | tf_op jit(solution)/shard_map/ppermute | solution.py:31
  260.2 2.8 add_convert_fusion.1
  263.1 42.0 %collective-permute-done = bf16[512,512]{1,0:T(8,128)(2,1)S(1)} collective-permute-done((bf16[512,512]{1,0:T(8,128)(2,1)S(1)}, bf16[512,512]{1,0:T(8,128)(2,1)S(1)}, u32[]{:S(2)}, u32[]{:S(2)}) %collective-permute-start) | collective-permute-done | bytes 524320 | tf_op jit(solution)/shard_map/ppermute | solution.py:31
  306.4 4.8 %collective-permute-start.42 = (bf16[512,512]{1,0:T(8,128)(2,1)S(1)}, bf16[512,512]{1,0:T(8,128)(2,1)S(1)}, u32[]{:S(2)}, u32[]{:S(2)}) collective-permute-start(bf16[512,512]{1,0:T(8,128)(2,1)S(1)} %get-tuple-element.43), channel_id=1, source_target_pairs={{1,8},{8,1},{3,10},{10,3},{5,12},{12,5},{7,14},{14,7},{17,24},{24,... | collective-permute-start | bytes 1572872 | tf_op jit(solution)/shard_map/ppermute | solution.py:331
  314.8 3.6 collective-permute-done.42
  318.4 4.6 collective-permute-done.41
  329.5 2.3 slice.134
  335.3 4.8 %collective-permute-start.47 = (bf16[512,512]{1,0:T(8,128)(2,1)S(1)}, bf16[512,512]{1,0:T(8,128)(2,1)S(1)}, u32[]{:S(2)}, u32[]{:S(2)}) collective-permute-start(bf16[512,512]{1,0:T(8,128)(2,1)S(1)} %add_convert_fusion.2.refs_0_), channel_id=1, source_target_pairs={{0,8},{8,0},{1,9},{9,1},{2,10},{10,2},{3,11},{11,3},{4,12},{12,4},... | collective-permute-start | bytes 1572872 | tf_op jit(solution)/shard_map/ppermute | solution.py:18
  342.3 7.3 %collective-permute-done.46.refs_3_ = bf16[512,512]{1,0:T(8,128)(2,1)} collective-permute-done((bf16[512,512]{1,0:T(8,128)(2,1)S(1)}, bf16[512,512]{1,0:T(8,128)(2,1)}, u32[]{:S(2)}, u32[]{:S(2)}) %collective-permute-start.46) | collective-permute-done | bytes 524320 | tf_op jit(solution)/shard_map/ppermute | solution.py:18
  349.6 6.7 %collective-permute-start.65 = (bf16[2,256,1024]{2,1,0:T(8,128)(2,1)}, bf16[2,256,1024]{2,1,0:T(8,128)(2,1)S(1)}, u32[]{:S(2)}, u32[]{:S(2)}) collective-permute-start(bf16[2,256,1024]{2,1,0:T(8,128)(2,1)} %slice.135), channel_id=1, source_target_pairs={{0,65},{64,0},{1,64},{65,1},{2,67},{66,2},{3,66},{67,3},{4,69},{68... | collective-permute-start | bytes 3145736 | tf_op jit(solution)/shard_map/ppermute | solution.py:23
  360.6 7.5 %collective-permute-done.64.refs_16_.refs_3_ = bf16[2,256,1024]{2,1,0:T(8,128)(2,1)S(1)} collective-permute-done((bf16[2,256,1024]{2,1,0:T(8,128)(2,1)}, bf16[2,256,1024]{2,1,0:T(8,128)(2,1)S(1)}, u32[]{:S(2)}, u32[]{:S(2)}) %collective-permute-start.64) | collective-permute-done | bytes 1048608 | tf_op jit(solution)/shard_map/ppermute | solution.py:23
  370.2 12.1 %collective-permute-done.65.refs_17_.refs_4_ = bf16[2,256,1024]{2,1,0:T(8,128)(2,1)S(1)} collective-permute-done((bf16[2,256,1024]{2,1,0:T(8,128)(2,1)}, bf16[2,256,1024]{2,1,0:T(8,128)(2,1)S(1)}, u32[]{:S(2)}, u32[]{:S(2)}) %collective-permute-start.65) | collective-permute-done | bytes 1048608 | tf_op jit(solution)/shard_map/ppermute | solution.py:23
  385.8 13.1 %shard_map.84 = (bf16[512,1536]{1,0:T(8,128)(2,1)S(1)}, bf16[160,1024]{1,0:T(8,128)(2,1)S(1)}) custom-call(s32[40]{0:T(128)S(1)} %stack.325.index_ref, f32[8,512]{1,0:T(8,128)S(1)} %squeeze.27.gain_ref, bf16[512,512]{1,0:T(8,128)(2,1)S(1)} %add_convert_fusion.2.refs_0_, bf16[512,512]{1,0:T(8,128)(2,1)S(1)} %collective-permute-done.44.refs_1_, ...), custom_call_target="tpu_custom_call" | custom-call | flops 6442450944 | bytes 18874368 | tf_op jit(solution)/shard_map/pallas_call | solution.py:111
  403.6 10.3 %collective-permute-done.66.tail_ref = bf16[160,1024]{1,0:T(8,128)(2,1)} collective-permute-done((bf16[160,1024]{1,0:T(8,128)(2,1)S(1)}, bf16[160,1024]{1,0:T(8,128)(2,1)}, u32[]{:S(2)}, u32[]{:S(2)}) %collective-permute-start.66) | collective-permute-done | bytes 327712 | tf_op jit(solution)/shard_map/ppermute | solution.py:37
  415.3 18.9 %shard_map.85 = (bf16[4,512,512]{2,1,0:T(8,128)(2,1)S(1)}, bf16[4,512,512]{2,1,0:T(8,128)(2,1)S(1)}) custom-call(s32[18]{0:T(128)S(1)} %stack.316.index_ref, bf16[160,1024]{1,0:T(8,128)(2,1)} %collective-permute-done.66.tail_ref, bf16[512,1536]{1,0:T(8,128)(2,1)S(1)} %copy-done.30, f32[9,512]{1,0:T(8,128)S(1)} %slice.136.feat_ref, ...), custom_call_target="tpu_custom_call" | custom-call | flops 8589934592 | bytes 10485760 | tf_op jit(solution)/shard_map/pallas_call | solution.py:222
  435.0 3.8 collective-permute-done.68
  442.8 11.6 %collective-permute-done.71 = bf16[512,512]{1,0:T(8,128)(2,1)S(1)} collective-permute-done((bf16[512,512]{1,0:T(8,128)(2,1)S(1)}, bf16[512,512]{1,0:T(8,128)(2,1)S(1)}, u32[]{:S(2)}, u32[]{:S(2)}) %collective-permute-start.71) | collective-permute-done | bytes 524320 | tf_op jit(solution)/shard_map/ppermute | solution.py:18
  454.3 11.9 %collective-permute-done.70 = bf16[512,512]{1,0:T(8,128)(2,1)S(1)} collective-permute-done((bf16[512,512]{1,0:T(8,128)(2,1)S(1)}, bf16[512,512]{1,0:T(8,128)(2,1)S(1)}, u32[]{:S(2)}, u32[]{:S(2)}) %collective-permute-start.70) | collective-permute-done | bytes 524320 | tf_op jit(solution)/shard_map/ppermute | solution.py:18
  468.5 10.1 %collective-permute-done.72 = bf16[512,512]{1,0:T(8,128)(2,1)S(1)} collective-permute-done((bf16[512,512]{1,0:T(8,128)(2,1)S(1)}, bf16[512,512]{1,0:T(8,128)(2,1)S(1)}, u32[]{:S(2)}, u32[]{:S(2)}) %collective-permute-start.72) | collective-permute-done | bytes 524320 | tf_op jit(solution)/shard_map/ppermute | solution.py:31
  (238 shorter events, 93.5 us)
Async XLA Ops:
  1.6 25.0 %collective-permute-start.3 = (bf16[512,512]{1,0:T(8,128)(2,1)}, bf16[512,512]{1,0:T(8,128)(2,1)S(1)}, u32[]{:S(2)}, u32[]{:S(2)}) collective-permute-start(bf16[512,512]{1,0:T(8,128)(2,1)} %refs_0_.1), channel_id=1, source_target_pairs={{0,4},{2,6},{4,0},{6,2},{1,5},{3,7},{5,1},{7,3},{8,12},{10,14},{12... | collective-permute-start | bytes 1572872 | tf_op jit(solution)/shard_map/ppermute | solution.py:18
  9.1 34.9 %collective-permute-start.8 = (bf16[256,1536]{1,0:T(8,128)(2,1)S(1)}, bf16[256,1536]{1,0:T(8,128)(2,1)}, u32[]{:S(2)}, u32[]{:S(2)}) collective-permute-start(bf16[256,1536]{1,0:T(8,128)(2,1)S(1)} %copy.17.refs_8_), channel_id=1, source_target_pairs={{0,64},{64,0},{1,65},{65,1},{2,66},{66,2},{3,67},{67,3},{4,68},{68... | collective-permute-start | bytes 2359304 | tf_op jit(solution)/shard_map/ppermute | solution.py:18
  10.4 29.8 %collective-permute-start.4 = (bf16[512,512]{1,0:T(8,128)(2,1)S(1)}, bf16[512,512]{1,0:T(8,128)(2,1)}, u32[]{:S(2)}, u32[]{:S(2)}) collective-permute-start(bf16[512,512]{1,0:T(8,128)(2,1)S(1)} %copy-done), channel_id=1, source_target_pairs={{0,1},{1,0},{2,3},{3,2},{4,5},{5,4},{6,7},{7,6},{8,9},{9,8},{10,11... | collective-permute-start | bytes 1572872 | tf_op jit(solution)/shard_map/ppermute | solution.py:18
  13.0 33.4 %collective-permute-start.9 = (bf16[256,1536]{1,0:T(8,128)(2,1)S(1)}, bf16[256,1536]{1,0:T(8,128)(2,1)}, u32[]{:S(2)}, u32[]{:S(2)}) collective-permute-start(bf16[256,1536]{1,0:T(8,128)(2,1)S(1)} %copy.17.refs_8_), channel_id=1, source_target_pairs={{0,16},{16,32},{32,48},{48,0},{1,17},{17,33},{33,49},{49,1},{2,18}... | collective-permute-start | bytes 2359304 | tf_op jit(solution)/shard_map/ppermute | solution.py:18
  14.4 32.7 %collective-permute-start.10 = (bf16[256,1536]{1,0:T(8,128)(2,1)S(1)}, bf16[256,1536]{1,0:T(8,128)(2,1)}, u32[]{:S(2)}, u32[]{:S(2)}) collective-permute-start(bf16[256,1536]{1,0:T(8,128)(2,1)S(1)} %copy.17.refs_8_), channel_id=1, source_target_pairs={{0,48},{16,0},{32,16},{48,32},{1,49},{17,1},{33,17},{49,33},{2,50}... | collective-permute-start | bytes 2359304 | tf_op jit(solution)/shard_map/ppermute | solution.py:18
  26.6 21.3 %collective-permute-start.11 = (bf16[256,1536]{1,0:T(8,128)(2,1)S(1)}, bf16[256,1536]{1,0:T(8,128)(2,1)}, u32[]{:S(2)}, u32[]{:S(2)}) collective-permute-start(bf16[256,1536]{1,0:T(8,128)(2,1)S(1)} %copy.17.refs_8_), channel_id=1, source_target_pairs={{0,32},{16,48},{32,0},{48,16},{1,33},{17,49},{33,1},{49,17},{2,34}... | collective-permute-start | bytes 2359304 | tf_op jit(solution)/shard_map/ppermute | solution.py:18
  44.1 28.8 %collective-permute-start.51 = (bf16[256,2048]{1,0:T(8,128)(2,1)S(1)}, bf16[256,2048]{1,0:T(8,128)(2,1)}, u32[]{:S(2)}, u32[]{:S(2)}) collective-permute-start(bf16[256,2048]{1,0:T(8,128)(2,1)S(1)} %pad_maximum_fusion.2), channel_id=1, source_target_pairs={{1,8},{8,1},{3,10},{10,3},{5,12},{12,5},{7,14},{14,7},{17,24},{24,... | collective-permute-start | bytes 3145736 | tf_op jit(solution)/shard_map/ppermute | solution.py:31
  47.9 24.9 %collective-permute-start.7 = (bf16[512,512]{1,0:T(8,128)(2,1)}, bf16[512,512]{1,0:T(8,128)(2,1)S(1)}, u32[]{:S(2)}, u32[]{:S(2)}) collective-permute-start(bf16[512,512]{1,0:T(8,128)(2,1)} %collective-permute-done.4.refs_4_), channel_id=1, source_target_pairs={{0,4},{2,6},{4,0},{6,2},{1,5},{3,7},{5,1},{7,3},{8,12},{10,14},{12... | collective-permute-start | bytes 1572872 | tf_op jit(solution)/shard_map/ppermute | solution.py:18
  50.1 24.2 %collective-permute-start.12 = (bf16[256,768]{1,0:T(8,128)(2,1)S(1)}, bf16[256,768]{1,0:T(8,128)(2,1)S(1)}, u32[]{:S(2)}, u32[]{:S(2)}) collective-permute-start(bf16[256,768]{1,0:T(8,128)(2,1)S(1)} %slice.126), channel_id=1, source_target_pairs={{0,16},{16,32},{32,48},{48,0},{1,17},{17,33},{33,49},{49,1},{2,18}... | collective-permute-start | bytes 1179656 | tf_op jit(solution)/shard_map/ppermute | solution.py:18
  60.7 17.1 %collective-permute-start.14 = (bf16[256,768]{1,0:T(8,128)(2,1)S(1)}, bf16[256,768]{1,0:T(8,128)(2,1)}, u32[]{:S(2)}, u32[]{:S(2)}) collective-permute-start(bf16[256,768]{1,0:T(8,128)(2,1)S(1)} %slice.126), channel_id=1, source_target_pairs={{0,32},{16,48},{32,0},{48,16},{1,33},{17,49},{33,1},{49,17},{2,34}... | collective-permute-start | bytes 1179656 | tf_op jit(solution)/shard_map/ppermute | solution.py:18
  72.9 18.6 %collective-permute-start.17 = (bf16[256,768]{1,0:T(8,128)(2,1)S(1)}, bf16[256,768]{1,0:T(8,128)(2,1)S(1)}, u32[]{:S(2)}, u32[]{:S(2)}) collective-permute-start(bf16[256,768]{1,0:T(8,128)(2,1)S(1)} %slice.129), channel_id=1, source_target_pairs={{0,64},{64,0},{1,65},{65,1},{2,66},{66,2},{3,67},{67,3},{4,68},{68... | collective-permute-start | bytes 1179656 | tf_op jit(solution)/shard_map/ppermute | solution.py:18
  74.3 34.3 %collective-permute-start.19 = (bf16[256,1536]{1,0:T(8,128)(2,1)}, bf16[256,1536]{1,0:T(8,128)(2,1)S(1)}, u32[]{:S(2)}, u32[]{:S(2)}) collective-permute-start(bf16[256,1536]{1,0:T(8,128)(2,1)} %collective-permute-done.8.refs_9_), channel_id=1, source_target_pairs={{0,8},{8,0},{1,9},{9,1},{2,10},{10,2},{3,11},{11,3},{4,12},{12,4},... | collective-permute-start | bytes 2359304 | tf_op jit(solution)/shard_map/ppermute | solution.py:18
  75.4 33.3 %collective-permute-start.20 = (bf16[256,1536]{1,0:T(8,128)(2,1)}, bf16[256,1536]{1,0:T(8,128)(2,1)S(1)}, u32[]{:S(2)}, u32[]{:S(2)}) collective-permute-start(bf16[256,1536]{1,0:T(8,128)(2,1)} %collective-permute-done.9.refs_10_), channel_id=1, source_target_pairs={{0,8},{8,0},{1,9},{9,1},{2,10},{10,2},{3,11},{11,3},{4,12},{12,4},... | collective-permute-start | bytes 2359304 | tf_op jit(solution)/shard_map/ppermute | solution.py:18
  77.8 22.1 %collective-permute-start.16 = (bf16[256,768]{1,0:T(8,128)(2,1)S(1)}, bf16[256,768]{1,0:T(8,128)(2,1)S(1)}, u32[]{:S(2)}, u32[]{:S(2)}) collective-permute-start(bf16[256,768]{1,0:T(8,128)(2,1)S(1)} %slice.128), channel_id=1, source_target_pairs={{0,64},{64,0},{1,65},{65,1},{2,66},{66,2},{3,67},{67,3},{4,68},{68... | collective-permute-start | bytes 1179656 | tf_op jit(solution)/shard_map/ppermute | solution.py:18
  83.0 26.2 %collective-permute-start.21 = (bf16[256,1536]{1,0:T(8,128)(2,1)}, bf16[256,1536]{1,0:T(8,128)(2,1)S(1)}, u32[]{:S(2)}, u32[]{:S(2)}) collective-permute-start(bf16[256,1536]{1,0:T(8,128)(2,1)} %collective-permute-done.10.refs_11_), channel_id=1, source_target_pairs={{0,8},{8,0},{1,9},{9,1},{2,10},{10,2},{3,11},{11,3},{4,12},{12,4},... | collective-permute-start | bytes 2359304 | tf_op jit(solution)/shard_map/ppermute | solution.py:18
  91.5 17.8 %collective-permute-start.22 = (bf16[256,1536]{1,0:T(8,128)(2,1)}, bf16[256,1536]{1,0:T(8,128)(2,1)S(1)}, u32[]{:S(2)}, u32[]{:S(2)}) collective-permute-start(bf16[256,1536]{1,0:T(8,128)(2,1)} %collective-permute-done.11.refs_12_), channel_id=1, source_target_pairs={{0,8},{8,0},{1,9},{9,1},{2,10},{10,2},{3,11},{11,3},{4,12},{12,4},... | collective-permute-start | bytes 2359304 | tf_op jit(solution)/shard_map/ppermute | solution.py:18
  109.3 24.9 %collective-permute-start.32 = (bf16[2,512,256]{2,1,0:T(8,128)(2,1)S(1)}, bf16[2,512,256]{2,1,0:T(8,128)(2,1)}, u32[]{:S(2)}, u32[]{:S(2)}) collective-permute-start(bf16[2,512,256]{2,1,0:T(8,128)(2,1)S(1)} %pad_maximum_fusion.3.refs_0_), channel_id=1, source_target_pairs={{0,48},{16,0},{32,16},{48,32},{1,49},{17,1},{33,17},{49,33},{2,50}... | collective-permute-start | bytes 1572872 | tf_op jit(solution)/shard_map/ppermute | solution.py:18
  112.1 23.0 %collective-permute-start.28 = (bf16[256,768]{1,0:T(8,128)(2,1)}, bf16[256,768]{1,0:T(8,128)(2,1)S(1)}, u32[]{:S(2)}, u32[]{:S(2)}) collective-permute-start(bf16[256,768]{1,0:T(8,128)(2,1)} %copy-done.23), channel_id=1, source_target_pairs={{0,8},{8,0},{1,9},{9,1},{2,10},{10,2},{3,11},{11,3},{4,12},{12,4},... | collective-permute-start | bytes 1179656 | tf_op jit(solution)/shard_map/ppermute | solution.py:18
  114.6 37.2 %collective-permute-start.33 = (bf16[2,512,256]{2,1,0:T(8,128)(2,1)S(1)}, bf16[2,512,256]{2,1,0:T(8,128)(2,1)}, u32[]{:S(2)}, u32[]{:S(2)}) collective-permute-start(bf16[2,512,256]{2,1,0:T(8,128)(2,1)S(1)} %pad_maximum_fusion.3.refs_0_), channel_id=1, source_target_pairs={{0,32},{16,48},{32,0},{48,16},{1,33},{17,49},{33,1},{49,17},{2,34}... | collective-permute-start | bytes 1572872 | tf_op jit(solution)/shard_map/ppermute | solution.py:18
  114.8 39.1 %collective-permute-start.34 = (bf16[2,512,256]{2,1,0:T(8,128)(2,1)S(1)}, bf16[2,512,256]{2,1,0:T(8,128)(2,1)S(1)}, u32[]{:S(2)}, u32[]{:S(2)}) collective-permute-start(bf16[2,512,256]{2,1,0:T(8,128)(2,1)S(1)} %pad_maximum_fusion.3.refs_0_), channel_id=1, source_target_pairs={{0,8},{8,0},{1,9},{9,1},{2,10},{10,2},{3,11},{11,3},{4,12},{12,4},... | collective-permute-start | bytes 1572872 | tf_op jit(solution)/shard_map/ppermute | solution.py:18
  122.9 34.2 %collective-permute-start.35 = (bf16[2,512,256]{2,1,0:T(8,128)(2,1)}, bf16[2,512,256]{2,1,0:T(8,128)(2,1)S(1)}, u32[]{:S(2)}, u32[]{:S(2)}) collective-permute-start(bf16[2,512,256]{2,1,0:T(8,128)(2,1)} %collective-permute-done.31.refs_1_), channel_id=1, source_target_pairs={{0,8},{8,0},{1,9},{9,1},{2,10},{10,2},{3,11},{11,3},{4,12},{12,4},... | collective-permute-start | bytes 1572872 | tf_op jit(solution)/shard_map/ppermute | solution.py:18
  134.2 23.9 %collective-permute-start.36 = (bf16[2,512,256]{2,1,0:T(8,128)(2,1)}, bf16[2,512,256]{2,1,0:T(8,128)(2,1)}, u32[]{:S(2)}, u32[]{:S(2)}) collective-permute-start(bf16[2,512,256]{2,1,0:T(8,128)(2,1)} %collective-permute-done.32.refs_2_), channel_id=1, source_target_pairs={{0,8},{8,0},{1,9},{9,1},{2,10},{10,2},{3,11},{11,3},{4,12},{12,4},... | collective-permute-start | bytes 1572872 | tf_op jit(solution)/shard_map/ppermute | solution.py:18
  153.9 17.1 %collective-permute-start.54 = (bf16[256,1024]{1,0:T(8,128)(2,1)}, bf16[256,1024]{1,0:T(8,128)(2,1)}, u32[]{:S(2)}, u32[]{:S(2)}) collective-permute-start(bf16[256,1024]{1,0:T(8,128)(2,1)} %get-tuple-element.41), channel_id=1, source_target_pairs={{0,1},{64,65},{1,0},{65,64},{2,3},{66,67},{3,2},{67,66},{4,5},{68,... | collective-permute-start | bytes 1572872 | tf_op jit(solution)/shard_map/ppermute | solution.py:23
  154.7 25.0 %collective-permute-start.53 = (bf16[256,1024]{1,0:T(8,128)(2,1)}, bf16[256,1024]{1,0:T(8,128)(2,1)}, u32[]{:S(2)}, u32[]{:S(2)}) collective-permute-start(bf16[256,1024]{1,0:T(8,128)(2,1)} %get-tuple-element.41), channel_id=1, source_target_pairs={{0,65},{64,0},{1,64},{65,1},{2,67},{66,2},{3,66},{67,3},{4,69},{68... | collective-permute-start | bytes 1572872 | tf_op jit(solution)/shard_map/ppermute | solution.py:23
  157.9 25.1 %collective-permute-start.52 = (bf16[256,1024]{1,0:T(8,128)(2,1)}, bf16[256,1024]{1,0:T(8,128)(2,1)}, u32[]{:S(2)}, u32[]{:S(2)}) collective-permute-start(bf16[256,1024]{1,0:T(8,128)(2,1)} %get-tuple-element.41), channel_id=1, source_target_pairs={{0,64},{64,1},{1,65},{65,0},{2,66},{66,3},{3,67},{67,2},{4,68},{68... | collective-permute-start | bytes 1572872 | tf_op jit(solution)/shard_map/ppermute | solution.py:23
  158.1 28.0 %collective-permute-start.61 = (bf16[256,1024]{1,0:T(8,128)(2,1)}, bf16[256,1024]{1,0:T(8,128)(2,1)S(1)}, u32[]{:S(2)}, u32[]{:S(2)}) collective-permute-start(bf16[256,1024]{1,0:T(8,128)(2,1)} %get-tuple-element.40), channel_id=1, source_target_pairs={{0,32},{16,48},{32,0},{48,16},{1,33},{17,49},{33,1},{49,17},{2,34}... | collective-permute-start | bytes 1572872 | tf_op jit(solution)/shard_map/ppermute | solution.py:18
  159.8 30.1 %collective-permute-start.60 = (bf16[256,1024]{1,0:T(8,128)(2,1)}, bf16[256,1024]{1,0:T(8,128)(2,1)S(1)}, u32[]{:S(2)}, u32[]{:S(2)}) collective-permute-start(bf16[256,1024]{1,0:T(8,128)(2,1)} %get-tuple-element.40), channel_id=1, source_target_pairs={{0,48},{16,0},{32,16},{48,32},{1,49},{17,1},{33,17},{49,33},{2,50}... | collective-permute-start | bytes 1572872 | tf_op jit(solution)/shard_map/ppermute | solution.py:18
  171.0 76.6 %collective-permute-start.40 = (bf16[512,1024]{1,0:T(8,128)(2,1)S(1)}, bf16[512,1024]{1,0:T(8,128)(2,1)S(1)}, u32[]{:S(2)}, u32[]{:S(2)}) collective-permute-start(bf16[512,1024]{1,0:T(8,128)(2,1)S(1)} %get-tuple-element.23), channel_id=1, source_target_pairs={{0,4},{2,6},{4,0},{6,2},{1,5},{3,7},{5,1},{7,3},{8,12},{10,14},{12... | collective-permute-start | bytes 3145736 | tf_op jit(solution)/shard_map/ppermute | solution.py:18
  179.7 73.1 %collective-permute-start.39 = (bf16[512,1024]{1,0:T(8,128)(2,1)S(1)}, bf16[512,1024]{1,0:T(8,128)(2,1)S(1)}, u32[]{:S(2)}, u32[]{:S(2)}) collective-permute-start(bf16[512,1024]{1,0:T(8,128)(2,1)S(1)} %get-tuple-element.22), channel_id=1, source_target_pairs={{0,6},{2,0},{4,2},{6,4},{1,7},{3,1},{5,3},{7,5},{8,14},{10,8},{12,... | collective-permute-start | bytes 3145736 | tf_op jit(solution)/shard_map/ppermute | solution.py:18
  183.0 71.2 %collective-permute-start.38 = (bf16[512,1024]{1,0:T(8,128)(2,1)S(1)}, bf16[512,1024]{1,0:T(8,128)(2,1)}, u32[]{:S(2)}, u32[]{:S(2)}) collective-permute-start(bf16[512,1024]{1,0:T(8,128)(2,1)S(1)} %get-tuple-element.21), channel_id=1, source_target_pairs={{0,2},{2,4},{4,6},{6,0},{1,3},{3,5},{5,7},{7,1},{8,10},{10,12},{12... | collective-permute-start | bytes 3145736 | tf_op jit(solution)/shard_map/ppermute | solution.py:18
  186.1 120.3 %collective-permute-start.55 = (bf16[4,256,1024]{2,1,0:T(8,128)(2,1)}, bf16[4,256,1024]{2,1,0:T(8,128)(2,1)}, u32[]{:S(2)}, u32[]{:S(2)}) collective-permute-start(bf16[4,256,1024]{2,1,0:T(8,128)(2,1)} %pad_maximum_fusion.refs_8_), channel_id=1, source_target_pairs={{0,16},{16,32},{32,48},{48,0},{1,17},{17,33},{33,49},{49,1},{2,18}... | collective-permute-start | bytes 6291464 | tf_op jit(solution)/shard_map/ppermute | solution.py:18
  189.9 55.2 %collective-permute-start.59 = (bf16[256,1024]{1,0:T(8,128)(2,1)}, bf16[256,1024]{1,0:T(8,128)(2,1)S(1)}, u32[]{:S(2)}, u32[]{:S(2)}) collective-permute-start(bf16[256,1024]{1,0:T(8,128)(2,1)} %get-tuple-element.40), channel_id=1, source_target_pairs={{0,16},{16,32},{32,48},{48,0},{1,17},{17,33},{33,49},{49,1},{2,18}... | collective-permute-start | bytes 1572872 | tf_op jit(solution)/shard_map/ppermute | solution.py:18
  245.0 78.5 %collective-permute-start.56 = (bf16[4,256,1024]{2,1,0:T(8,128)(2,1)}, bf16[4,256,1024]{2,1,0:T(8,128)(2,1)}, u32[]{:S(2)}, u32[]{:S(2)}) collective-permute-start(bf16[4,256,1024]{2,1,0:T(8,128)(2,1)} %pad_maximum_fusion.refs_8_), channel_id=1, source_target_pairs={{0,48},{16,0},{32,16},{48,32},{1,49},{17,1},{33,17},{49,33},{2,50}... | collective-permute-start | bytes 6291464 | tf_op jit(solution)/shard_map/ppermute | solution.py:18
  247.7 80.4 %collective-permute-start.62 = (bf16[4,256,1024]{2,1,0:T(8,128)(2,1)}, bf16[4,256,1024]{2,1,0:T(8,128)(2,1)}, u32[]{:S(2)}, u32[]{:S(2)}) collective-permute-start(bf16[4,256,1024]{2,1,0:T(8,128)(2,1)} %pad_maximum_fusion.1.refs_13_.refs_0_), channel_id=1, source_target_pairs={{0,64},{64,1},{1,65},{65,0},{2,66},{66,3},{3,67},{67,2},{4,68},{68... | collective-permute-start | bytes 6291464 | tf_op jit(solution)/shard_map/ppermute | solution.py:23
  253.8 74.3 %collective-permute-start.63 = (bf16[4,256,1024]{2,1,0:T(8,128)(2,1)}, bf16[4,256,1024]{2,1,0:T(8,128)(2,1)}, u32[]{:S(2)}, u32[]{:S(2)}) collective-permute-start(bf16[4,256,1024]{2,1,0:T(8,128)(2,1)} %pad_maximum_fusion.1.refs_13_.refs_0_), channel_id=1, source_target_pairs={{0,65},{64,0},{1,64},{65,1},{2,67},{66,2},{3,66},{67,3},{4,69},{68... | collective-permute-start | bytes 6291464 | tf_op jit(solution)/shard_map/ppermute | solution.py:23
  254.2 50.9 %collective-permute-start = (bf16[512,512]{1,0:T(8,128)(2,1)S(1)}, bf16[512,512]{1,0:T(8,128)(2,1)S(1)}, u32[]{:S(2)}, u32[]{:S(2)}) collective-permute-start(bf16[512,512]{1,0:T(8,128)(2,1)S(1)} %copy-done), channel_id=1, source_target_pairs={{1,8},{8,1},{3,10},{10,3},{5,12},{12,5},{7,14},{14,7},{17,24},{24,... | collective-permute-start | bytes 1572872 | tf_op jit(solution)/shard_map/ppermute | solution.py:31
  326.3 23.3 %collective-permute-start.46 = (bf16[512,512]{1,0:T(8,128)(2,1)S(1)}, bf16[512,512]{1,0:T(8,128)(2,1)}, u32[]{:S(2)}, u32[]{:S(2)}) collective-permute-start(bf16[512,512]{1,0:T(8,128)(2,1)S(1)} %add_convert_fusion.2.refs_0_), channel_id=1, source_target_pairs={{0,4},{2,6},{4,0},{6,2},{1,5},{3,7},{5,1},{7,3},{8,12},{10,14},{12... | collective-permute-start | bytes 1572872 | tf_op jit(solution)/shard_map/ppermute | solution.py:18
  328.0 29.1 %collective-permute-start.57 = (bf16[2,256,1024]{2,1,0:T(8,128)(2,1)S(1)}, bf16[2,256,1024]{2,1,0:T(8,128)(2,1)S(1)}, u32[]{:S(2)}, u32[]{:S(2)}) collective-permute-start(bf16[2,256,1024]{2,1,0:T(8,128)(2,1)S(1)} %slice.132), channel_id=1, source_target_pairs={{0,16},{16,32},{32,48},{48,0},{1,17},{17,33},{33,49},{49,1},{2,18}... | collective-permute-start | bytes 3145736 | tf_op jit(solution)/shard_map/ppermute | solution.py:18
  328.1 30.6 %collective-permute-start.58 = (bf16[2,256,1024]{2,1,0:T(8,128)(2,1)S(1)}, bf16[2,256,1024]{2,1,0:T(8,128)(2,1)S(1)}, u32[]{:S(2)}, u32[]{:S(2)}) collective-permute-start(bf16[2,256,1024]{2,1,0:T(8,128)(2,1)S(1)} %slice.133), channel_id=1, source_target_pairs={{0,48},{16,0},{32,16},{48,32},{1,49},{17,1},{33,17},{49,33},{2,50}... | collective-permute-start | bytes 3145736 | tf_op jit(solution)/shard_map/ppermute | solution.py:18
  335.3 21.1 %collective-permute-start.47 = (bf16[512,512]{1,0:T(8,128)(2,1)S(1)}, bf16[512,512]{1,0:T(8,128)(2,1)S(1)}, u32[]{:S(2)}, u32[]{:S(2)}) collective-permute-start(bf16[512,512]{1,0:T(8,128)(2,1)S(1)} %add_convert_fusion.2.refs_0_), channel_id=1, source_target_pairs={{0,8},{8,0},{1,9},{9,1},{2,10},{10,2},{3,11},{11,3},{4,12},{12,4},... | collective-permute-start | bytes 1572872 | tf_op jit(solution)/shard_map/ppermute | solution.py:18
  340.1 28.0 %collective-permute-start.64 = (bf16[2,256,1024]{2,1,0:T(8,128)(2,1)}, bf16[2,256,1024]{2,1,0:T(8,128)(2,1)S(1)}, u32[]{:S(2)}, u32[]{:S(2)}) collective-permute-start(bf16[2,256,1024]{2,1,0:T(8,128)(2,1)} %slice.134), channel_id=1, source_target_pairs={{0,64},{64,1},{1,65},{65,0},{2,66},{66,3},{3,67},{67,2},{4,68},{68... | collective-permute-start | bytes 3145736 | tf_op jit(solution)/shard_map/ppermute | solution.py:23
  349.6 32.7 %collective-permute-start.65 = (bf16[2,256,1024]{2,1,0:T(8,128)(2,1)}, bf16[2,256,1024]{2,1,0:T(8,128)(2,1)S(1)}, u32[]{:S(2)}, u32[]{:S(2)}) collective-permute-start(bf16[2,256,1024]{2,1,0:T(8,128)(2,1)} %slice.135), channel_id=1, source_target_pairs={{0,65},{64,0},{1,64},{65,1},{2,67},{66,2},{3,66},{67,3},{4,69},{68... | collective-permute-start | bytes 3145736 | tf_op jit(solution)/shard_map/ppermute | solution.py:23
  357.2 25.2 %collective-permute-start.48 = (bf16[512,512]{1,0:T(8,128)(2,1)S(1)}, bf16[512,512]{1,0:T(8,128)(2,1)}, u32[]{:S(2)}, u32[]{:S(2)}) collective-permute-start(bf16[512,512]{1,0:T(8,128)(2,1)S(1)} %collective-permute-done.44.refs_1_), channel_id=1, source_target_pairs={{0,8},{8,0},{1,9},{9,1},{2,10},{10,2},{3,11},{11,3},{4,12},{12,4},... | collective-permute-start | bytes 1572872 | tf_op jit(solution)/shard_map/ppermute | solution.py:18
  358.2 24.2 %collective-permute-start.49 = (bf16[512,512]{1,0:T(8,128)(2,1)}, bf16[512,512]{1,0:T(8,128)(2,1)}, u32[]{:S(2)}, u32[]{:S(2)}) collective-permute-start(bf16[512,512]{1,0:T(8,128)(2,1)} %collective-permute-done.45.refs_2_), channel_id=1, source_target_pairs={{0,8},{8,0},{1,9},{9,1},{2,10},{10,2},{3,11},{11,3},{4,12},{12,4},... | collective-permute-start | bytes 1572872 | tf_op jit(solution)/shard_map/ppermute | solution.py:18
  359.7 22.7 %collective-permute-start.50 = (bf16[512,512]{1,0:T(8,128)(2,1)}, bf16[512,512]{1,0:T(8,128)(2,1)}, u32[]{:S(2)}, u32[]{:S(2)}) collective-permute-start(bf16[512,512]{1,0:T(8,128)(2,1)} %collective-permute-done.46.refs_3_), channel_id=1, source_target_pairs={{0,8},{8,0},{1,9},{9,1},{2,10},{10,2},{3,11},{11,3},{4,12},{12,4},... | collective-permute-start | bytes 1572872 | tf_op jit(solution)/shard_map/ppermute | solution.py:18
  368.1 34.3 %collective-permute-start.67 = (f32[138,512]{1,0:T(8,128)}, f32[138,512]{1,0:T(8,128)}, u32[]{:S(2)}, u32[]{:S(2)}) collective-permute-start(f32[138,512]{1,0:T(8,128)} %pad_maximum_fusion.4), channel_id=1, source_target_pairs={{1,8},{8,1},{3,10},{10,3},{5,12},{12,5},{7,14},{14,7},{17,24},{24,... | collective-permute-start | bytes 847880 | tf_op jit(solution)/shard_map/ppermute | solution.py:31
  441.3 24.9 %collective-permute-start.70 = (bf16[512,512]{1,0:T(8,128)(2,1)S(1)}, bf16[512,512]{1,0:T(8,128)(2,1)S(1)}, u32[]{:S(2)}, u32[]{:S(2)}) collective-permute-start(bf16[512,512]{1,0:T(8,128)(2,1)S(1)} %get-tuple-element.35), channel_id=1, source_target_pairs={{0,6},{2,0},{4,2},{6,4},{1,7},{3,1},{5,3},{7,5},{8,14},{10,8},{12,... | collective-permute-start | bytes 1572872 | tf_op jit(solution)/shard_map/ppermute | solution.py:18
  441.3 24.9 %collective-permute-start.69 = (bf16[512,512]{1,0:T(8,128)(2,1)S(1)}, bf16[512,512]{1,0:T(8,128)(2,1)S(1)}, u32[]{:S(2)}, u32[]{:S(2)}) collective-permute-start(bf16[512,512]{1,0:T(8,128)(2,1)S(1)} %get-tuple-element.33), channel_id=1, source_target_pairs={{0,2},{2,4},{4,6},{6,0},{1,3},{3,5},{5,7},{7,1},{8,10},{10,12},{12... | collective-permute-start | bytes 1572872 | tf_op jit(solution)/shard_map/ppermute | solution.py:18
  (71 other events, 956.6 us)

commit v3 on v2

--- a/solution.py
+++ b/solution.py
@@ -4,6 +4,7 @@
 import jax.numpy as jnp
 import numpy as np
 from jax import lax
+from jax.experimental.layout import Layout, with_layout_constraint
 from jax.experimental import pallas as pl
 from jax.experimental.pallas import tpu as pltpu
 from jax.sharding import Mesh, PartitionSpec as P
@@ -11,16 +12,12 @@
 AXES = ("xl", "y", "core", "z", "xh")
 ROWS = 512
 LANES = 128
+CUT = 1152
 
 
 def shift(value, axis, by):
     size = lax.axis_size(axis)
     return lax.ppermute(value, axis, [(i, (i + by) % size) for i in range(size)])
-
-
-def shift_x(value, by):
-    place = lambda x: (x % 2) * 2 + x // 2
-    return lax.ppermute(value, ("xl", "xh"), [(place(x), place((x + by) % 4)) for x in range(4)])
 
 
 def shift_y(value, by):
@@ -37,22 +34,18 @@
     return lax.ppermute(value, axes, [(i, i + 1) for i in range(15)])
 
 
+def by_rows(value):
+    return with_layout_constraint(value, Layout(major_to_minor=tuple(range(value.ndim))))
+
+
 def after(value, *others):
     return lax.optimization_barrier((value, *others))[0]
 
 
-def ring_four(value, move):
-    one = move(value, 1)
-    three = move(value, -1)
-    low = move(one[:2], 1)
-    high = move(three[2:], -1)
-    return one, three, low, high
-
-
 def fetch(moves, sources, target, index_ref, semaphores):
     copies = []
-    for number, (source, lead, lane, width, slot, other, by_rows) in enumerate(moves):
-        block = pl.multiple_of(index_ref[slot] * 256, 256)
+    for number, (source, lead, lane, width, slot, other, by_rows, *fixed) in enumerate(moves):
+        block = fixed[0] * 256 if slot is None else pl.multiple_of(index_ref[slot] * 256, 256)
         ref = sources[source]
         if lead is not None:
             ref = ref.at[lead]
@@ -64,12 +57,15 @@
     return copies
 
 
-def in_kernel(moves, pieces, halo, index_ref, gain_ref, *refs):
+def in_kernel(x_moves, moves, pieces, halo, index_ref, gain_ref, *refs):
     xs, refs = refs[:pieces], refs[pieces:]
     count = 1 + max(m[0] for m in moves)
     ws, refs = refs[:count], refs[count:]
     out_ref, tail_ref, raw, normed, weights, squares, x_sems, w_sems = refs
-    loads = [pltpu.make_async_copy(x, raw.at[j], x_sems.at[j]) for j, x in enumerate(xs)]
+    loads = []
+    for j, (source, lead, _) in enumerate(x_moves):
+        x = xs[source] if lead is None else xs[source].at[lead]
+        loads.append(pltpu.make_async_copy(x, raw.at[j], x_sems.at[j]))
     for load in loads:
         load.start()
     copies = fetch(moves, ws, weights, index_ref, w_sems)
@@ -78,7 +74,7 @@
     squares[...] = jnp.zeros_like(squares)
     for j, load in enumerate(loads):
         load.wait()
-        block = index_ref[j]
+        block = x_moves[j][2] if x_moves[j][1] is not None else index_ref[j]
         lanes = pl.ds(pl.multiple_of(block * 512, 512), 512)
         gain = gain_ref[pl.ds(block, 1), :]
 
@@ -105,11 +101,11 @@
     tail_ref[halo:, 512:] = jnp.zeros((16, 512), jnp.bfloat16)
 
 
-def project_in(index, gain, pieces, weights, moves, halo):
+def project_in(index, gain, pieces, x_moves, weights, moves, halo):
     any_space = pl.BlockSpec(memory_space=pl.ANY)
     vmem = pl.BlockSpec(memory_space=pltpu.VMEM)
     return pl.pallas_call(
-        functools.partial(in_kernel, moves, len(pieces), halo),
+        functools.partial(in_kernel, x_moves, moves, len(pieces), halo),
         out_shape=[
             jax.ShapeDtypeStruct((ROWS, 1536), jnp.bfloat16),
             jax.ShapeDtypeStruct((halo + 16, 1024), jnp.bfloat16),
@@ -117,11 +113,11 @@
         in_specs=[pl.BlockSpec(memory_space=pltpu.SMEM), vmem] + [any_space] * (len(pieces) + len(weights)),
         out_specs=[vmem, vmem],
         scratch_shapes=[
-            pltpu.VMEM((len(pieces), ROWS, 512), jnp.bfloat16),
+            pltpu.VMEM((8, ROWS, 512), jnp.bfloat16),
             pltpu.VMEM((ROWS, 4096), jnp.bfloat16),
             pltpu.VMEM((4096, 1536), jnp.bfloat16),
             pltpu.VMEM((ROWS, LANES), jnp.float32),
-            pltpu.SemaphoreType.DMA((len(pieces),)),
+            pltpu.SemaphoreType.DMA((8,)),
             pltpu.SemaphoreType.DMA((len(moves),)),
         ],
         compiler_params=pltpu.CompilerParams(vmem_limit_bytes=44 * 1024 * 1024),
@@ -196,8 +192,8 @@
 
     for copy in copies:
         copy.wait()
-    z = index_ref[16]
-    core = index_ref[17]
+    z = index_ref[0]
+    core = index_ref[1]
     for by in range(4):
         block = lax.rem(z + by, 4)
         if outs == 4:
@@ -241,84 +237,56 @@
 
 def per_device(hidden, norm_gain, in_weight, feat_filter, se_filter, mr_filter, skip_gain, out_weight):
     xl, y, core, z, xh = (lax.axis_index(a) for a in AXES)
-    x = 2 * xh + xl
     behind = lambda place, by: (place - by) % 4
     gains = norm_gain.reshape(2, 8, 512)
-
-    partner = shift(hidden, "xh", 1)
-    x_pieces, x_slots = [hidden], [z * 2 + xh]
-    for by in (1, -1, 2):
-        x_pieces.append(shift(hidden, "z", by))
-        x_slots.append(behind(z, by) * 2 + xh)
-    w = in_weight[0].reshape(256, 1536)
-    w_xl = shift(w, "xl", 1)
-    w_y = {by: shift_y(w, by) for by in (1, -1, 2)}
-    x_pieces.append(partner)
-    x_slots.append(z * 2 + 1 - xh)
-    for by in (1, -1, 2):
-        x_pieces.append(shift(partner, "z", by))
-        x_slots.append(behind(z, by) * 2 + 1 - xh)
-
-    held = [(w, xl, y, 0, 1536), (w_xl, 1 - xl, y, 0, 1536)]
-    held += [(w_y[by], xl, behind(y, by), 0, 1536) for by in (1, -1, 2)]
-    held += [(shift_y(w_xl[:, :768], by), 1 - xl, behind(y, by), 0, 768) for by in (1, -1, 2)]
-    held += [(shift(w_y[by][:, 768:], "xl", 1), 1 - xl, behind(y, by), 768, 768) for by in (1, -1, 2)]
-    w_list, w_moves, w_slots = [], [], []
-    for c, get in ((core, lambda v: v), (1 - core, lambda v: shift(v, "core", 1))):
-        for value, at_xl, at_y, lane, width in held:
-            w_moves.append((len(w_list), None, 0, width, 8 + len(w_slots), lane, True))
-            w_list.append(get(value))
-            w_slots.append(at_xl * 8 + at_y * 2 + c)
-    index = jnp.stack(x_slots + w_slots).astype(jnp.int32)
-    projected, tail = project_in(index, gains[0], x_pieces, w_list, w_moves, 16)
-
-    o = after(out_weight[0], w_list[8], w_list[10])
-    o_duo = jnp.stack([o, shift(o, "xl", 1)])
-    o_held = [o_duo] + [shift_y(o_duo, by) for by in (1, -1, 2)]
-    o_list, o_moves, o_slots = [], [], []
-    for c, get in ((core, lambda v: v), (1 - core, lambda v: shift(v, "core", 1))):
-        for value, by in zip(o_held, (0, 1, -1, 2)):
-            for e in range(2):
-                o_moves.append((len(o_list), e, 0, 256, len(o_slots), 0, False))
-                o_slots.append((xl if e == 0 else 1 - xl) * 8 + behind(y, by) * 2 + c)
-            o_list.append(get(value))
-    o_index = jnp.stack(o_slots + [z, core]).astype(jnp.int32)
-
-    small = swap(jnp.concatenate([feat_filter[1].reshape(9, 512), skip_gain[1:2], mr_filter], axis=0))
-    m = jnp.concatenate(
-        [in_weight[1].reshape(256, 1536), out_weight[1, :256], out_weight[1, 256:]], axis=1
-    )
-    m = after(swap(m), w_list[8], w_list[10])
-    a, b = m[:, :1024], m[:, 1024:]
-    a4 = jnp.stack([a] + [shift_x(a, by) for by in (1, -1, 2)])
-    b4 = jnp.stack([b] + [shift_y(b, by) for by in (1, -1, 2)])
-    a_lists = (a4,) + ring_four(a4, shift_y)
-    b_lists = (b4,) + ring_four(b4, shift_x)
     hops = (0, 1, -1, 2)
-    block_of = lambda at_x, at_y: (at_x % 2) * 8 + at_y * 2 + at_x // 2
+
+    def side_by_side(layer):
+        return jnp.concatenate(
+            [in_weight[layer].reshape(256, 1536), out_weight[layer, :256], out_weight[layer, 256:]], axis=1
+        )
+
+    whole = lax.all_gather(hidden, ("z", "xh"), axis=0, tiled=False)
+
+    m = side_by_side(0)
+    m_y = {by: shift_y(m, by) for by in (1, -1, 2)}
+    m_xl = shift(m, "xl", 1)
+    held = [(m, xl, y, 0, 2048), (m_xl, 1 - xl, y, 0, 2048)]
+    held += [(m_y[by], xl, behind(y, by), 0, 2048) for by in (1, -1, 2)]
+    rest = shift(jnp.stack([m_y[by][:, CUT:] for by in (1, -1, 2)]), "xl", 1)
+    held += [(shift_y(m_xl[:, :CUT], by), 1 - xl, behind(y, by), 0, CUT) for by in (1, -1, 2)]
     w_list, w_moves, w_slots = [], [], []
     q_list, q_moves, q_slots = [], [], []
-    for is_b, lists in ((False, a_lists), (True, b_lists)):
-        for value, by, entries in zip(lists, (0, 1, -1, 2, 2), (range(4), range(4), range(4), (0, 1), (2, 3))):
-            for lead, e in enumerate(entries):
-                near, far = (y, x) if is_b else (x, y)
-                near, far = behind(near, hops[e]), behind(far, by)
-                slot = block_of(far, near) if is_b else block_of(near, far)
-                if is_b:
-                    w_moves.append((len(w_list), lead, 0, 512, 8 + len(w_slots), 1024, True))
-                    for half in range(2):
-                        q_moves.append((len(q_list), lead, 512 + 256 * half, 256, len(q_slots), 256 * half, False))
-                    q_slots.append(slot)
-                else:
-                    w_moves.append((len(w_list), lead, 0, 1024, 8 + len(w_slots), 0, True))
-                w_slots.append(slot)
+    for c, get in ((core, lambda v: v), (1 - core, lambda v: shift(v, "core", 1))):
+        ready = [(get(value), None, *where) for value, *where in held]
+        value = get(rest)
+        ready += [(value, e, 1 - xl, behind(y, by), CUT, 2048) for e, by in enumerate((1, -1, 2))]
+        for value, lead, at_xl, at_y, low, high in ready:
+            slot = at_xl * 8 + at_y * 2 + c
+            w_moves.append((len(w_list), lead, 0, min(high, 1536) - low, len(w_slots), low, True))
             w_list.append(value)
-            if is_b:
+            w_slots.append(slot)
+            if high == 2048:
+                for half in range(2):
+                    q_moves.append((len(q_list), lead, 1536 + 256 * half - low, 256, 2 + len(q_slots), 256 * half, False))
                 q_list.append(value)
-
+                q_slots.append(slot)
+    w_index = jnp.stack(w_slots).astype(jnp.int32)
+    q_index = jnp.stack([z, core] + q_slots).astype(jnp.int32)
+
+    m = swap(by_rows(after(side_by_side(1), m_xl, *m_y.values())))
+    m = after(m, *w_list[5:9])
+    w1 = by_rows(lax.all_gather(by_rows(m[:, :1536]), ("xh", "xl", "y"), axis=0, tiled=False))
+    o1 = by_rows(lax.all_gather(by_rows(m[:, 1536:]), ("xh", "xl", "y"), axis=0, tiled=False))
+    small, base = jnp.concatenate([feat_filter[1].reshape(9, 512), skip_gain[1:2], mr_filter], axis=0), hidden
+    small, base = after((small, base), *w_list[5:9])
+    small, base = swap(small), swap(base)
+
+    x_moves = [(0, j, j) for j in range(8)]
+    projected, tail = project_in(w_index, gains[0], [whole], x_moves, w_list, w_moves, 16)
     tail = from_behind(tail, ("xl", "y", "core"))
     parts = mix_out(
-        o_index, tail, projected, feat_filter[0].reshape(9, 512), se_filter, skip_gain[0:1], o_list, o_moves, 16,
+        q_index, tail, projected, feat_filter[0].reshape(9, 512), se_filter, skip_gain[0:1], q_list, q_moves, 16,
         [(ROWS, 1024)] * 4,
     )
     total = parts[0].astype(jnp.float32)
@@ -331,7 +299,7 @@
     second = lax.ppermute(others, ("core", "xh"), [(1, 2), (2, 1)])
     third = lax.ppermute(others, ("core", "xh"), [(0, 2), (3, 1)])
     kept = jnp.where(core == xh, mine, jnp.zeros_like(mine))
-    current = swap(hidden).astype(jnp.float32) + kept.astype(jnp.float32)
+    current = base.astype(jnp.float32) + kept.astype(jnp.float32)
     for value in (first, second, third):
         current = current + value.astype(jnp.float32)
     current = current.astype(jnp.bfloat16)
@@ -342,12 +310,15 @@
         for value, by in zip(values, hops):
             x_pieces.append(value)
             x_slots.append(behind(z, by) * 2 + side)
-    index = jnp.stack(x_slots + w_slots).astype(jnp.int32)
-    projected, tail = project_in(index, gains[1], x_pieces, w_list, w_moves, 144)
+    index = jnp.stack(x_slots).astype(jnp.int32)
+    places = [(p, (p // 4 % 2) * 8 + (p % 4) * 2 + p // 8) for p in range(16)]
+    x_moves = [(j, None, j) for j in range(8)]
+    w_moves = [(0, p, 0, 1536, None, 0, True, block) for p, block in places]
+    projected, tail = project_in(index, gains[1], x_pieces, x_moves, [w1], w_moves, 144)
     tail = from_behind(tail, ("xl", "y", "xh"))
-    q_slots = q_slots + [z, core]
+    q_moves = [(0, p, 256 * half, 256, None, 256 * half, False, block) for p, block in places for half in range(2)]
     own, theirs = mix_out(
-        jnp.stack(q_slots).astype(jnp.int32), tail, projected, small[:9], small[10:], small[9:10], q_list, q_moves, 144,
+        jnp.stack([z, core]).astype(jnp.int32), tail, projected, small[:9], small[10:], small[9:10], [o1], q_moves, 144,
         [(4, ROWS, 512)] * 2,
     )
     both = (own.astype(jnp.float32) + shift(theirs, "core", 1).astype(jnp.float32)).astype(jnp.bfloat16)

time: 489 us -> 371 us (0.76)
  the two profiles are of different devices: /device:TPU:41 before, /device:TPU:1 now
where the time goes in v3:
time: 371 us; the launch traced here: 368 us
  waiting for transfers between devices  188 us (51%)
  starting transfers between devices  77 us (21%)
  Pallas kernels  54.5 us (15%)
  local copies, waits for them, and re-layouts  23.1 us (6%)
  between operations  13.6 us (4%)
  other arithmetic  12.6 us (3%)
    ppermute x31, waiting for transfers between devices, shift(): lax.ppermute(value, axis, [(i, (i + by) % size) for i in range(size)])  136 us
    ppermute x31, starting transfers between devices, shift(): lax.ppermute(value, axis, [(i, (i + by) % size) for i in range(size)])  44.2 us
    ppermute x4, waiting for transfers between devices, swap(): moved = lax.ppermute(value, ('core', 'xh'), [(1, 2), (2, 1)])  33.9 us
    pallas_call x2, Pallas kernels, project_in(): pl.pallas_call(functools.partial(in_kernel, x_moves, moves, len(pieces),...  28.4 us
    pallas_call x2, Pallas kernels, mix_out(): pl.pallas_call(functools.partial(mix_kernel, moves, halo, length, len(out...  26.1 us
    ppermute x4, starting transfers between devices, swap(): moved = lax.ppermute(value, ('core', 'xh'), [(1, 2), (2, 1)])  20.4 us
    unnamed x34, local copies, waits for them, and re-layouts  11.7 us
    ppermute x1, waiting for transfers between devices, per_device(): first = lax.ppermute(mine, ('core', 'xh'), [(1, 0), (2, 3)])  7.78 us
  transfers between devices with their start and end apart: 43, of which 20 were waited for; matrix products, arithmetic and copies ran while one was open for 7% of the time, Pallas kernels for 10%

profile of v3, /device:TPU:1, one launch (start us, length us, event | category | flops | bytes accessed | tf_op | source)
XLA Modules:
  0.0 368.2 jit_solution(17033704300865191123)
XLA Ops:
  7.3 2.4 fusion.4
  10.9 2.1 collective-permute-start
  15.8 1.6 collective-permute-start.6
  17.4 2.3 copy.18
  19.7 2.3 copy.14
  22.1 2.4 pad_maximum_fusion.2
  24.4 16.7 %collective-permute-done.refs_2_.refs_1_ = bf16[256,2048]{1,0:T(8,128)(2,1)S(1)} collective-permute-done((bf16[256,2048]{1,0:T(8,128)(2,1)S(1)}, bf16[256,2048]{1,0:T(8,128)(2,1)S(1)}, u32[]{:S(2)}, u32[]{:S(2)}) %collective-permute-start) | collective-permute-done | bytes 1048608 | tf_op jit(solution)/shard_map/ppermute | solution.py:20
  41.2 20.6 %collective-permute-done.6.refs_5_.refs_4_ = bf16[256,2048]{1,0:T(8,128)(2,1)} collective-permute-done((bf16[256,2048]{1,0:T(8,128)(2,1)S(1)}, bf16[256,2048]{1,0:T(8,128)(2,1)}, u32[]{:S(2)}, u32[]{:S(2)}) %collective-permute-start.6) | collective-permute-done | bytes 1048608 | tf_op jit(solution)/shard_map/ppermute | solution.py:20
  61.8 6.1 %collective-permute-start.32 = (bf16[256,2048]{1,0:T(8,128)(2,1)}, bf16[256,2048]{1,0:T(8,128)(2,1)}, u32[]{:S(2)}, u32[]{:S(2)}) collective-permute-start(bf16[256,2048]{1,0:T(8,128)(2,1)} %pad_maximum_fusion.2), channel_id=1, source_target_pairs={{1,8},{8,1},{3,10},{10,3},{5,12},{12,5},{7,14},{14,7},{17,24},{24,... | collective-permute-start | bytes 3145736 | tf_op jit(solution)/shard_map/ppermute | solution.py:28
  73.1 1.8 collective-permute-start.2
  74.9 27.0 %collective-permute-done.32 = bf16[256,2048]{1,0:T(8,128)(2,1)} collective-permute-done((bf16[256,2048]{1,0:T(8,128)(2,1)}, bf16[256,2048]{1,0:T(8,128)(2,1)}, u32[]{:S(2)}, u32[]{:S(2)}) %collective-permute-start.32) | collective-permute-done | bytes 1048608 | tf_op jit(solution)/shard_map/ppermute | solution.py:28
  103.4 15.9 %collective-permute-done.7.refs_9_.refs_10_.refs_11_.refs_5_.refs_6_.refs_7_ = bf16[3,256,896]{2,1,0:T(8,128)(2,1)} collective-permute-done((bf16[3,256,896]{2,1,0:T(8,128)(2,1)}, bf16[3,256,896]{2,1,0:T(8,128)(2,1)}, u32[]{:S(2)}, u32[]{:S(2)}) %collective-permute-start.7) | collective-permute-done | bytes 1376288 | tf_op jit(solution)/shard_map/ppermute | solution.py:20
  120.3 1.7 slice.109
  123.2 1.5 collective-permute-done.9.refs_12_.refs_8_
  125.9 3.4 collective-permute-done.10.refs_13_.refs_9_
  129.4 2.9 collective-permute-done.11.refs_14_.refs_10_
  134.8 1.8 collective-permute-done.16.refs_19_
  137.8 14.8 %shard_map.82 = (bf16[512,1536]{1,0:T(8,128)(2,1)}, bf16[32,1024]{1,0:T(8,128)(2,1)S(1)}) custom-call(s32[22]{0:T(128)S(1)} %stack.149.index_ref, f32[8,512]{1,0:T(8,128)S(1)} %squeeze.30.gain_ref, bf16[8,512,512]{2,1,0:T(8,128)(2,1)} %bitcast.56, bf16[256,2048]{1,0:T(8,128)(2,1)S(1)} %pad_maximum_fusion.1.refs_1_.refs_0_, ...), custom_call_target="tpu_custom_call" | custom-call | flops 6442450944 | bytes 18874368 | tf_op jit(solution)/shard_map/pallas_call | solution.py:107
  152.6 3.3 collective-permute-start.18
  157.1 7.9 %shard_map.83 = (bf16[512,1024]{1,0:T(8,128)(2,1)S(1)}, bf16[512,1024]{1,0:T(8,128)(2,1)}, bf16[512,1024]{1,0:T(8,128)(2,1)}, bf16[512,1024]{1,0:T(8,128)(2,1)}) custom-call(s32[18]{0:T(128)S(1)} %stack.148.index_ref, bf16[32,1024]{1,0:T(8,128)(2,1)S(1)} %collective-permute-done.18.tail_ref, bf16[512,1536]{1,0:T(8,128)(2,1)} %get-tuple-element.21.main_ref, ...), custom_call_target="tpu_custom_call" | custom-call | flops 2147483648 | bytes 10485760 | tf_op jit(solution)/shard_map/pallas_call | solution.py:218
  166.0 2.9 collective-permute-start.21
  170.3 1.7 pad_maximum_fusion.3
  172.0 4.4 %collective-permute-start.8 = (bf16[512,512]{1,0:T(8,128)(2,1)}, bf16[512,512]{1,0:T(8,128)(2,1)S(1)}, u32[]{:S(2)}, u32[]{:S(2)}) collective-permute-start(bf16[512,512]{1,0:T(8,128)(2,1)} %param.8), channel_id=1, source_target_pairs={{1,8},{8,1},{3,10},{10,3},{5,12},{12,5},{7,14},{14,7},{17,24},{24,... | collective-permute-start | bytes 1572872 | tf_op jit(solution)/shard_map/ppermute | solution.py:28
  176.4 16.2 %collective-permute-done.21 = bf16[512,1024]{1,0:T(8,128)(2,1)S(1)} collective-permute-done((bf16[512,1024]{1,0:T(8,128)(2,1)}, bf16[512,1024]{1,0:T(8,128)(2,1)S(1)}, u32[]{:S(2)}, u32[]{:S(2)}) %collective-permute-start.21) | collective-permute-done | bytes 1048608 | tf_op jit(solution)/shard_map/ppermute | solution.py:20
  192.6 22.7 %collective-permute-done.20 = bf16[512,1024]{1,0:T(8,128)(2,1)S(1)} collective-permute-done((bf16[512,1024]{1,0:T(8,128)(2,1)}, bf16[512,1024]{1,0:T(8,128)(2,1)S(1)}, u32[]{:S(2)}, u32[]{:S(2)}) %collective-permute-start.20) | collective-permute-done | bytes 1048608 | tf_op jit(solution)/shard_map/ppermute | solution.py:20
  216.3 2.4 add_convert_fusion.1
  220.3 4.5 %collective-permute-start.23 = (bf16[512,512]{1,0:T(8,128)(2,1)S(1)}, bf16[512,512]{1,0:T(8,128)(2,1)S(1)}, u32[]{:S(2)}, u32[]{:S(2)}) collective-permute-start(bf16[512,512]{1,0:T(8,128)(2,1)S(1)} %get-tuple-element.43), channel_id=1, source_target_pairs={{1,8},{8,1},{3,10},{10,3},{5,12},{12,5},{7,14},{14,7},{17,24},{24,... | collective-permute-start | bytes 1572872 | tf_op jit(solution)/shard_map/ppermute | solution.py:299
  224.7 1.5 collective-permute-start.22
  226.2 6.0 %collective-permute-done.23 = bf16[512,512]{1,0:T(8,128)(2,1)S(1)} collective-permute-done((bf16[512,512]{1,0:T(8,128)(2,1)S(1)}, bf16[512,512]{1,0:T(8,128)(2,1)S(1)}, u32[]{:S(2)}, u32[]{:S(2)}) %collective-permute-start.23) | collective-permute-done | bytes 524320 | tf_op jit(solution)/shard_map/ppermute | solution.py:299
  232.3 7.8 %collective-permute-done.22 = bf16[512,512]{1,0:T(8,128)(2,1)S(1)} collective-permute-done((bf16[512,512]{1,0:T(8,128)(2,1)S(1)}, bf16[512,512]{1,0:T(8,128)(2,1)S(1)}, u32[]{:S(2)}, u32[]{:S(2)}) %collective-permute-start.22) | collective-permute-done | bytes 524320 | tf_op jit(solution)/shard_map/ppermute | solution.py:298
  241.6 1.7 collective-permute-start.26
  244.6 2.2 collective-permute-start.28
  246.8 6.9 %collective-permute-done.25.refs_1_ = bf16[512,512]{1,0:T(8,128)(2,1)S(1)} collective-permute-done((bf16[512,512]{1,0:T(8,128)(2,1)S(1)}, bf16[512,512]{1,0:T(8,128)(2,1)S(1)}, u32[]{:S(2)}, u32[]{:S(2)}) %collective-permute-start.25) | collective-permute-done | bytes 524320 | tf_op jit(solution)/shard_map/ppermute | solution.py:20
  253.7 3.4 collective-permute-start.29
  257.1 9.5 %collective-permute-start.30 = (bf16[512,512]{1,0:T(8,128)(2,1)S(1)}, bf16[512,512]{1,0:T(8,128)(2,1)}, u32[]{:S(2)}, u32[]{:S(2)}) collective-permute-start(bf16[512,512]{1,0:T(8,128)(2,1)S(1)} %collective-permute-done.26.refs_2_), channel_id=1, source_target_pairs={{0,8},{8,0},{1,9},{9,1},{2,10},{10,2},{3,11},{11,3},{4,12},{12,4},... | collective-permute-start | bytes 1572872 | tf_op jit(solution)/shard_map/ppermute | solution.py:20
  266.7 1.6 collective-permute-start.31
  268.3 2.7 collective-permute-start.34
  271.1 13.6 %shard_map.84 = (bf16[512,1536]{1,0:T(8,128)(2,1)S(1)}, bf16[160,1024]{1,0:T(8,128)(2,1)S(1)}) custom-call(s32[8]{0:T(128)S(1)} %stack.159.index_ref, f32[8,512]{1,0:T(8,128)S(1)} %squeeze.31.gain_ref, bf16[512,512]{1,0:T(8,128)(2,1)S(1)} %add_convert_fusion.2.refs_0_, bf16[512,512]{1,0:T(8,128)(2,1)S(1)} %collective-permute-done.25.refs_1_, ...), custom_call_target="tpu_custom_call" | custom-call | flops 6442450944 | bytes 18874368 | tf_op jit(solution)/shard_map/pallas_call | solution.py:107
  285.9 1.7 collective-permute-start.33
  288.8 2.6 collective-permute-done.33.tail_ref
  292.8 18.2 %shard_map.85 = (bf16[4,512,512]{2,1,0:T(8,128)(2,1)S(1)}, bf16[4,512,512]{2,1,0:T(8,128)(2,1)S(1)}) custom-call(s32[2]{0:T(128)S(1)} %pad_add_fusion.index_ref, bf16[160,1024]{1,0:T(8,128)(2,1)S(1)} %collective-permute-done.33.tail_ref, bf16[512,1536]{1,0:T(8,128)(2,1)S(1)} %copy-done.5, f32[9,512]{1,0:T(8,128)S(1)} %slice.120.feat_ref, ...), custom_call_target="tpu_custom_call" | custom-call | flops 8589934592 | bytes 10485760 | tf_op jit(solution)/shard_map/pallas_call | solution.py:218
  311.0 4.0 %collective-permute-start.35 = (bf16[4,512,512]{2,1,0:T(8,128)(2,1)S(1)}, bf16[4,512,512]{2,1,0:T(8,128)(2,1)S(1)}, u32[]{:S(2)}, u32[]{:S(2)}) collective-permute-start(bf16[4,512,512]{2,1,0:T(8,128)(2,1)S(1)} %get-tuple-element.32), channel_id=1, source_target_pairs={{0,8},{8,0},{1,9},{9,1},{2,10},{10,2},{3,11},{11,3},{4,12},{12,4},... | collective-permute-start | bytes 6291464 | tf_op jit(solution)/shard_map/ppermute | solution.py:20
  315.0 3.8 %collective-permute-done.35 = bf16[4,512,512]{2,1,0:T(8,128)(2,1)S(1)} collective-permute-done((bf16[4,512,512]{2,1,0:T(8,128)(2,1)S(1)}, bf16[4,512,512]{2,1,0:T(8,128)(2,1)S(1)}, u32[]{:S(2)}, u32[]{:S(2)}) %collective-permute-start.35) | collective-permute-done | bytes 2097184 | tf_op jit(solution)/shard_map/ppermute | solution.py:20
  320.5 2.9 collective-permute-start.37
  323.5 10.7 %collective-permute-done.38 = bf16[512,512]{1,0:T(8,128)(2,1)S(1)} collective-permute-done((bf16[512,512]{1,0:T(8,128)(2,1)S(1)}, bf16[512,512]{1,0:T(8,128)(2,1)S(1)}, u32[]{:S(2)}, u32[]{:S(2)}) %collective-permute-start.38) | collective-permute-done | bytes 524320 | tf_op jit(solution)/shard_map/ppermute | solution.py:20
  334.2 12.2 %collective-permute-done.37 = bf16[512,512]{1,0:T(8,128)(2,1)S(1)} collective-permute-done((bf16[512,512]{1,0:T(8,128)(2,1)S(1)}, bf16[512,512]{1,0:T(8,128)(2,1)S(1)}, u32[]{:S(2)}, u32[]{:S(2)}) %collective-permute-start.37) | collective-permute-done | bytes 524320 | tf_op jit(solution)/shard_map/ppermute | solution.py:20
  346.8 7.2 %collective-permute-start.39 = (bf16[512,512]{1,0:T(8,128)(2,1)S(1)}, bf16[512,512]{1,0:T(8,128)(2,1)S(1)}, u32[]{:S(2)}, u32[]{:S(2)}) collective-permute-start(bf16[512,512]{1,0:T(8,128)(2,1)S(1)} %fusion.3), channel_id=1, source_target_pairs={{1,8},{8,1},{3,10},{10,3},{5,12},{12,5},{7,14},{14,7},{17,24},{24,... | collective-permute-start | bytes 1572872 | tf_op jit(solution)/shard_map/ppermute | solution.py:28
  354.0 6.8 %collective-permute-done.39 = bf16[512,512]{1,0:T(8,128)(2,1)S(1)} collective-permute-done((bf16[512,512]{1,0:T(8,128)(2,1)S(1)}, bf16[512,512]{1,0:T(8,128)(2,1)S(1)}, u32[]{:S(2)}, u32[]{:S(2)}) %collective-permute-start.39) | collective-permute-done | bytes 524320 | tf_op jit(solution)/shard_map/ppermute | solution.py:28
  (116 shorter events, 34.3 us)
Async XLA Ops:
  6.5 130.1 %all-gather.7.cloned.1.call-start = ((), (), s32[]{:S(2)}) async-start(), calls=%async_computation | async-start | bytes 4718592 | tf_op jit(solution)/shard_map/all_gather | solution.py:249
  7.3 263.8 %all-gather.9.cloned.1.call-start = ((), (), s32[]{:S(2)}) async-start(), calls=%async_computation.1 | async-start | bytes 13369344 | tf_op jit(solution)/shard_map/all_gather | solution.py:279
  10.9 30.2 %collective-permute-start = (bf16[256,2048]{1,0:T(8,128)(2,1)S(1)}, bf16[256,2048]{1,0:T(8,128)(2,1)S(1)}, u32[]{:S(2)}, u32[]{:S(2)}) collective-permute-start(bf16[256,2048]{1,0:T(8,128)(2,1)S(1)} %pad_maximum_fusion.1.refs_1_.refs_0_), channel_id=1, source_target_pairs={{0,64},{64,0},{1,65},{65,1},{2,66},{66,2},{3,67},{67,3},{4,68},{68... | collective-permute-start | bytes 3145736 | tf_op jit(solution)/shard_map/ppermute | solution.py:20
  13.1 28.1 %collective-permute-start.4 = (bf16[256,2048]{1,0:T(8,128)(2,1)S(1)}, bf16[256,2048]{1,0:T(8,128)(2,1)S(1)}, u32[]{:S(2)}, u32[]{:S(2)}) collective-permute-start(bf16[256,2048]{1,0:T(8,128)(2,1)S(1)} %pad_maximum_fusion.1.refs_1_.refs_0_), channel_id=1, source_target_pairs={{0,16},{16,32},{32,48},{48,0},{1,17},{17,33},{33,49},{49,1},{2,18}... | collective-permute-start | bytes 3145736 | tf_op jit(solution)/shard_map/ppermute | solution.py:20
  14.4 26.8 %collective-permute-start.5 = (bf16[256,2048]{1,0:T(8,128)(2,1)S(1)}, bf16[256,2048]{1,0:T(8,128)(2,1)}, u32[]{:S(2)}, u32[]{:S(2)}) collective-permute-start(bf16[256,2048]{1,0:T(8,128)(2,1)S(1)} %pad_maximum_fusion.1.refs_1_.refs_0_), channel_id=1, source_target_pairs={{0,48},{16,0},{32,16},{48,32},{1,49},{17,1},{33,17},{49,33},{2,50}... | collective-permute-start | bytes 3145736 | tf_op jit(solution)/shard_map/ppermute | solution.py:20
  15.8 46.0 %collective-permute-start.6 = (bf16[256,2048]{1,0:T(8,128)(2,1)S(1)}, bf16[256,2048]{1,0:T(8,128)(2,1)}, u32[]{:S(2)}, u32[]{:S(2)}) collective-permute-start(bf16[256,2048]{1,0:T(8,128)(2,1)S(1)} %pad_maximum_fusion.1.refs_1_.refs_0_), channel_id=1, source_target_pairs={{0,32},{16,48},{32,0},{48,16},{1,33},{17,49},{33,1},{49,17},{2,34}... | collective-permute-start | bytes 3145736 | tf_op jit(solution)/shard_map/ppermute | solution.py:20
  61.8 40.2 %collective-permute-start.32 = (bf16[256,2048]{1,0:T(8,128)(2,1)}, bf16[256,2048]{1,0:T(8,128)(2,1)}, u32[]{:S(2)}, u32[]{:S(2)}) collective-permute-start(bf16[256,2048]{1,0:T(8,128)(2,1)} %pad_maximum_fusion.2), channel_id=1, source_target_pairs={{1,8},{8,1},{3,10},{10,3},{5,12},{12,5},{7,14},{14,7},{17,24},{24,... | collective-permute-start | bytes 3145736 | tf_op jit(solution)/shard_map/ppermute | solution.py:28
  71.4 47.9 %collective-permute-start.7 = (bf16[3,256,896]{2,1,0:T(8,128)(2,1)}, bf16[3,256,896]{2,1,0:T(8,128)(2,1)}, u32[]{:S(2)}, u32[]{:S(2)}) collective-permute-start(bf16[3,256,896]{2,1,0:T(8,128)(2,1)} %pad_maximum_fusion), channel_id=1, source_target_pairs={{0,64},{64,0},{1,65},{65,1},{2,66},{66,2},{3,67},{67,3},{4,68},{68... | collective-permute-start | bytes 4128776 | tf_op jit(solution)/shard_map/ppermute | solution.py:20
  72.2 31.1 %collective-permute-start.1 = (bf16[256,1152]{1,0:T(8,128)(2,1)}, bf16[256,1152]{1,0:T(8,128)(2,1)}, u32[]{:S(2)}, u32[]{:S(2)}) collective-permute-start(bf16[256,1152]{1,0:T(8,128)(2,1)} %slice.114), channel_id=1, source_target_pairs={{0,16},{16,32},{32,48},{48,0},{1,17},{17,33},{33,49},{49,1},{2,18}... | collective-permute-start | bytes 1769480 | tf_op jit(solution)/shard_map/ppermute | solution.py:20
  73.1 30.3 %collective-permute-start.2 = (bf16[256,1152]{1,0:T(8,128)(2,1)}, bf16[256,1152]{1,0:T(8,128)(2,1)}, u32[]{:S(2)}, u32[]{:S(2)}) collective-permute-start(bf16[256,1152]{1,0:T(8,128)(2,1)} %slice.114), channel_id=1, source_target_pairs={{0,48},{16,0},{32,16},{48,32},{1,49},{17,1},{33,17},{49,33},{2,50}... | collective-permute-start | bytes 1769480 | tf_op jit(solution)/shard_map/ppermute | solution.py:20
  74.9 28.5 %collective-permute-start.3 = (bf16[256,1152]{1,0:T(8,128)(2,1)}, bf16[256,1152]{1,0:T(8,128)(2,1)}, u32[]{:S(2)}, u32[]{:S(2)}) collective-permute-start(bf16[256,1152]{1,0:T(8,128)(2,1)} %slice.114), channel_id=1, source_target_pairs={{0,32},{16,48},{32,0},{48,16},{1,33},{17,49},{33,1},{49,17},{2,34}... | collective-permute-start | bytes 1769480 | tf_op jit(solution)/shard_map/ppermute | solution.py:20
  103.3 31.0 %copy-start.14 = (f32[2,4096]{1,0:T(2,128)S(1)}, f32[2,4096]{1,0:T(2,128)}, u32[]{:S(2)}) copy-start(f32[2,4096]{1,0:T(2,128)} %param.9) | copy-start | bytes 98308
  103.3 31.2 %copy-start.15 = (f32[2,512]{1,0:T(2,128)S(1)}, f32[2,512]{1,0:T(2,128)}, u32[]{:S(2)}) copy-start(f32[2,512]{1,0:T(2,128)} %param.14) | copy-start | bytes 12292
  120.3 168.5 %all-gather.11.cloned.1.call-start = ((), (), s32[]{:S(2)}) async-start(), calls=%async_computation.2 | async-start | bytes 4456448 | tf_op jit(solution)/shard_map/all_gather | solution.py:280
  122.0 2.7 collective-permute-start.9
  122.1 7.1 %collective-permute-start.10 = (bf16[256,2048]{1,0:T(8,128)(2,1)S(1)}, bf16[256,2048]{1,0:T(8,128)(2,1)S(1)}, u32[]{:S(2)}, u32[]{:S(2)}) collective-permute-start(bf16[256,2048]{1,0:T(8,128)(2,1)S(1)} %collective-permute-done.refs_2_.refs_1_), channel_id=1, source_target_pairs={{0,8},{8,0},{1,9},{9,1},{2,10},{10,2},{3,11},{11,3},{4,12},{12,4},... | collective-permute-start | bytes 3145736 | tf_op jit(solution)/shard_map/ppermute | solution.py:20
  122.6 9.6 %collective-permute-start.11 = (bf16[256,2048]{1,0:T(8,128)(2,1)S(1)}, bf16[256,2048]{1,0:T(8,128)(2,1)S(1)}, u32[]{:S(2)}, u32[]{:S(2)}) collective-permute-start(bf16[256,2048]{1,0:T(8,128)(2,1)S(1)} %collective-permute-done.4.refs_3_.refs_2_), channel_id=1, source_target_pairs={{0,8},{8,0},{1,9},{9,1},{2,10},{10,2},{3,11},{11,3},{4,12},{12,4},... | collective-permute-start | bytes 3145736 | tf_op jit(solution)/shard_map/ppermute | solution.py:20
  122.7 10.5 %collective-permute-start.12 = (bf16[256,2048]{1,0:T(8,128)(2,1)}, bf16[256,2048]{1,0:T(8,128)(2,1)S(1)}, u32[]{:S(2)}, u32[]{:S(2)}) collective-permute-start(bf16[256,2048]{1,0:T(8,128)(2,1)} %collective-permute-done.5.refs_4_.refs_3_), channel_id=1, source_target_pairs={{0,8},{8,0},{1,9},{9,1},{2,10},{10,2},{3,11},{11,3},{4,12},{12,4},... | collective-permute-start | bytes 3145736 | tf_op jit(solution)/shard_map/ppermute | solution.py:20
  123.1 13.5 %collective-permute-start.17 = (bf16[3,256,896]{2,1,0:T(8,128)(2,1)}, bf16[3,256,896]{2,1,0:T(8,128)(2,1)}, u32[]{:S(2)}, u32[]{:S(2)}) collective-permute-start(bf16[3,256,896]{2,1,0:T(8,128)(2,1)} %collective-permute-done.7.refs_9_.refs_10_.refs_11_.refs_5_.refs_6_.refs_7_), channel_id=1, source_target_pairs={{0,8},{8,0},{1,9},{9,1},{2,10},{10,2},{3,11},{11,3},{4,12},{12,4},... | collective-permute-start | bytes 4128776 | tf_op jit(solution)/shard_map/ppermute | solution.py:20
  125.8 8.8 %collective-permute-start.13 = (bf16[256,2048]{1,0:T(8,128)(2,1)}, bf16[256,2048]{1,0:T(8,128)(2,1)}, u32[]{:S(2)}, u32[]{:S(2)}) collective-permute-start(bf16[256,2048]{1,0:T(8,128)(2,1)} %collective-permute-done.6.refs_5_.refs_4_), channel_id=1, source_target_pairs={{0,8},{8,0},{1,9},{9,1},{2,10},{10,2},{3,11},{11,3},{4,12},{12,4},... | collective-permute-start | bytes 3145736 | tf_op jit(solution)/shard_map/ppermute | solution.py:20
  129.3 5.4 %collective-permute-start.14 = (bf16[256,1152]{1,0:T(8,128)(2,1)}, bf16[256,1152]{1,0:T(8,128)(2,1)}, u32[]{:S(2)}, u32[]{:S(2)}) collective-permute-start(bf16[256,1152]{1,0:T(8,128)(2,1)} %collective-permute-done.1.refs_6_), channel_id=1, source_target_pairs={{0,8},{8,0},{1,9},{9,1},{2,10},{10,2},{3,11},{11,3},{4,12},{12,4},... | collective-permute-start | bytes 1769480 | tf_op jit(solution)/shard_map/ppermute | solution.py:20
  132.3 2.5 collective-permute-start.15
  134.2 2.3 collective-permute-start.16
  137.8 18.1 %copy-start.13 = (f32[2,3,3,512]{3,0,2,1:T(2,128)S(1)}, f32[2,3,3,512]{3,0,2,1:T(2,128)}, u32[]{:S(2)}) copy-start(f32[2,3,3,512]{3,0,2,1:T(2,128)} %param.11) | copy-start | bytes 110596
  137.8 19.3 %copy-start.3 = (f32[7,512]{1,0:T(8,128)S(1)}, f32[7,512]{1,0:T(8,128)}, u32[]{:S(2)}) copy-start(f32[7,512]{1,0:T(8,128)} %filter_ref.1) | copy-start | bytes 43012
  152.6 4.4 %collective-permute-start.18 = (bf16[32,1024]{1,0:T(8,128)(2,1)S(1)}, bf16[32,1024]{1,0:T(8,128)(2,1)S(1)}, u32[]{:S(2)}, u32[]{:S(2)}) collective-permute-start(bf16[32,1024]{1,0:T(8,128)(2,1)S(1)} %get-tuple-element.20), channel_id=1, source_target_pairs={{0,8},{8,16},{16,24},{24,32},{32,40},{40,48},{48,56},{56,64},{64,7... | collective-permute-start | bytes 196616 | tf_op jit(solution)/shard_map/ppermute | solution.py:34
  166.0 26.6 %collective-permute-start.21 = (bf16[512,1024]{1,0:T(8,128)(2,1)}, bf16[512,1024]{1,0:T(8,128)(2,1)S(1)}, u32[]{:S(2)}, u32[]{:S(2)}) collective-permute-start(bf16[512,1024]{1,0:T(8,128)(2,1)} %get-tuple-element.25), channel_id=1, source_target_pairs={{0,4},{2,6},{4,0},{6,2},{1,5},{3,7},{5,1},{7,3},{8,12},{10,14},{12... | collective-permute-start | bytes 3145736 | tf_op jit(solution)/shard_map/ppermute | solution.py:20
  168.8 46.4 %collective-permute-start.20 = (bf16[512,1024]{1,0:T(8,128)(2,1)}, bf16[512,1024]{1,0:T(8,128)(2,1)S(1)}, u32[]{:S(2)}, u32[]{:S(2)}) collective-permute-start(bf16[512,1024]{1,0:T(8,128)(2,1)} %get-tuple-element.24), channel_id=1, source_target_pairs={{0,6},{2,0},{4,2},{6,4},{1,7},{3,1},{5,3},{7,5},{8,14},{10,8},{12,... | collective-permute-start | bytes 3145736 | tf_op jit(solution)/shard_map/ppermute | solution.py:20
  169.6 45.6 %collective-permute-start.19 = (bf16[512,1024]{1,0:T(8,128)(2,1)}, bf16[512,1024]{1,0:T(8,128)(2,1)S(1)}, u32[]{:S(2)}, u32[]{:S(2)}) collective-permute-start(bf16[512,1024]{1,0:T(8,128)(2,1)} %get-tuple-element.23), channel_id=1, source_target_pairs={{0,2},{2,4},{4,6},{6,0},{1,3},{3,5},{5,7},{7,1},{8,10},{10,12},{12... | collective-permute-start | bytes 3145736 | tf_op jit(solution)/shard_map/ppermute | solution.py:20
  172.0 54.2 %collective-permute-start.8 = (bf16[512,512]{1,0:T(8,128)(2,1)}, bf16[512,512]{1,0:T(8,128)(2,1)S(1)}, u32[]{:S(2)}, u32[]{:S(2)}) collective-permute-start(bf16[512,512]{1,0:T(8,128)(2,1)} %param.8), channel_id=1, source_target_pairs={{1,8},{8,1},{3,10},{10,3},{5,12},{12,5},{7,14},{14,7},{17,24},{24,... | collective-permute-start | bytes 1572872 | tf_op jit(solution)/shard_map/ppermute | solution.py:28
  218.7 21.3 %copy-start.10 = (bf16[512,512]{1,0:T(8,128)(2,1)S(1)}, bf16[512,512]{1,0:T(8,128)(2,1)}, u32[]{:S(2)}) copy-start(bf16[512,512]{1,0:T(8,128)(2,1)} %param.8) | copy-start | bytes 1572868
  218.8 7.4 %collective-permute-start.24 = (bf16[512,512]{1,0:T(8,128)(2,1)S(1)}, bf16[512,512]{1,0:T(8,128)(2,1)S(1)}, u32[]{:S(2)}, u32[]{:S(2)}) collective-permute-start(bf16[512,512]{1,0:T(8,128)(2,1)S(1)} %get-tuple-element.43), channel_id=1, source_target_pairs={{0,8},{9,1},{2,10},{11,3},{4,12},{13,5},{6,14},{15,7},{16,24},{25,... | collective-permute-start | bytes 1572872 | tf_op jit(solution)/shard_map/ppermute | solution.py:300
  220.3 12.0 %collective-permute-start.23 = (bf16[512,512]{1,0:T(8,128)(2,1)S(1)}, bf16[512,512]{1,0:T(8,128)(2,1)S(1)}, u32[]{:S(2)}, u32[]{:S(2)}) collective-permute-start(bf16[512,512]{1,0:T(8,128)(2,1)S(1)} %get-tuple-element.43), channel_id=1, source_target_pairs={{1,8},{8,1},{3,10},{10,3},{5,12},{12,5},{7,14},{14,7},{17,24},{24,... | collective-permute-start | bytes 1572872 | tf_op jit(solution)/shard_map/ppermute | solution.py:299
  224.7 15.3 %collective-permute-start.22 = (bf16[512,512]{1,0:T(8,128)(2,1)S(1)}, bf16[512,512]{1,0:T(8,128)(2,1)S(1)}, u32[]{:S(2)}, u32[]{:S(2)}) collective-permute-start(bf16[512,512]{1,0:T(8,128)(2,1)S(1)} %get-tuple-element.42), channel_id=1, source_target_pairs={{1,0},{8,9},{3,2},{10,11},{5,4},{12,13},{7,6},{14,15},{17,16},{24,... | collective-permute-start | bytes 1572872 | tf_op jit(solution)/shard_map/ppermute | solution.py:298
  240.5 13.2 %collective-permute-start.25 = (bf16[512,512]{1,0:T(8,128)(2,1)S(1)}, bf16[512,512]{1,0:T(8,128)(2,1)S(1)}, u32[]{:S(2)}, u32[]{:S(2)}) collective-permute-start(bf16[512,512]{1,0:T(8,128)(2,1)S(1)} %add_convert_fusion.2.refs_0_), channel_id=1, source_target_pairs={{0,2},{2,4},{4,6},{6,0},{1,3},{3,5},{5,7},{7,1},{8,10},{10,12},{12... | collective-permute-start | bytes 1572872 | tf_op jit(solution)/shard_map/ppermute | solution.py:20
  241.6 15.6 %collective-permute-start.26 = (bf16[512,512]{1,0:T(8,128)(2,1)S(1)}, bf16[512,512]{1,0:T(8,128)(2,1)S(1)}, u32[]{:S(2)}, u32[]{:S(2)}) collective-permute-start(bf16[512,512]{1,0:T(8,128)(2,1)S(1)} %add_convert_fusion.2.refs_0_), channel_id=1, source_target_pairs={{0,6},{2,0},{4,2},{6,4},{1,7},{3,1},{5,3},{7,5},{8,14},{10,8},{12,... | collective-permute-start | bytes 1572872 | tf_op jit(solution)/shard_map/ppermute | solution.py:20
  243.2 23.4 %collective-permute-start.27 = (bf16[512,512]{1,0:T(8,128)(2,1)S(1)}, bf16[512,512]{1,0:T(8,128)(2,1)S(1)}, u32[]{:S(2)}, u32[]{:S(2)}) collective-permute-start(bf16[512,512]{1,0:T(8,128)(2,1)S(1)} %add_convert_fusion.2.refs_0_), channel_id=1, source_target_pairs={{0,4},{2,6},{4,0},{6,2},{1,5},{3,7},{5,1},{7,3},{8,12},{10,14},{12... | collective-permute-start | bytes 1572872 | tf_op jit(solution)/shard_map/ppermute | solution.py:20
  244.6 26.4 %collective-permute-start.28 = (bf16[512,512]{1,0:T(8,128)(2,1)S(1)}, bf16[512,512]{1,0:T(8,128)(2,1)S(1)}, u32[]{:S(2)}, u32[]{:S(2)}) collective-permute-start(bf16[512,512]{1,0:T(8,128)(2,1)S(1)} %add_convert_fusion.2.refs_0_), channel_id=1, source_target_pairs={{0,8},{8,0},{1,9},{9,1},{2,10},{10,2},{3,11},{11,3},{4,12},{12,4},... | collective-permute-start | bytes 1572872 | tf_op jit(solution)/shard_map/ppermute | solution.py:20
  253.7 17.3 %collective-permute-start.29 = (bf16[512,512]{1,0:T(8,128)(2,1)S(1)}, bf16[512,512]{1,0:T(8,128)(2,1)S(1)}, u32[]{:S(2)}, u32[]{:S(2)}) collective-permute-start(bf16[512,512]{1,0:T(8,128)(2,1)S(1)} %collective-permute-done.25.refs_1_), channel_id=1, source_target_pairs={{0,8},{8,0},{1,9},{9,1},{2,10},{10,2},{3,11},{11,3},{4,12},{12,4},... | collective-permute-start | bytes 1572872 | tf_op jit(solution)/shard_map/ppermute | solution.py:20
  257.1 13.9 %collective-permute-start.30 = (bf16[512,512]{1,0:T(8,128)(2,1)S(1)}, bf16[512,512]{1,0:T(8,128)(2,1)}, u32[]{:S(2)}, u32[]{:S(2)}) collective-permute-start(bf16[512,512]{1,0:T(8,128)(2,1)S(1)} %collective-permute-done.26.refs_2_), channel_id=1, source_target_pairs={{0,8},{8,0},{1,9},{9,1},{2,10},{10,2},{3,11},{11,3},{4,12},{12,4},... | collective-permute-start | bytes 1572872 | tf_op jit(solution)/shard_map/ppermute | solution.py:20
  266.7 4.4 %collective-permute-start.31 = (bf16[512,512]{1,0:T(8,128)(2,1)S(1)}, bf16[512,512]{1,0:T(8,128)(2,1)}, u32[]{:S(2)}, u32[]{:S(2)}) collective-permute-start(bf16[512,512]{1,0:T(8,128)(2,1)S(1)} %collective-permute-done.27.refs_3_), channel_id=1, source_target_pairs={{0,8},{8,0},{1,9},{9,1},{2,10},{10,2},{3,11},{11,3},{4,12},{12,4},... | collective-permute-start | bytes 1572872 | tf_op jit(solution)/shard_map/ppermute | solution.py:20
  268.3 19.4 %collective-permute-start.34 = (f32[138,512]{1,0:T(8,128)}, f32[138,512]{1,0:T(8,128)}, u32[]{:S(2)}, u32[]{:S(2)}) collective-permute-start(f32[138,512]{1,0:T(8,128)} %pad_maximum_fusion.3), channel_id=1, source_target_pairs={{1,8},{8,1},{3,10},{10,3},{5,12},{12,5},{7,14},{14,7},{17,24},{24,... | collective-permute-start | bytes 847880 | tf_op jit(solution)/shard_map/ppermute | solution.py:28
  285.9 5.5 %collective-permute-start.33 = (bf16[160,1024]{1,0:T(8,128)(2,1)S(1)}, bf16[160,1024]{1,0:T(8,128)(2,1)S(1)}, u32[]{:S(2)}, u32[]{:S(2)}) collective-permute-start(bf16[160,1024]{1,0:T(8,128)(2,1)S(1)} %get-tuple-element.28), channel_id=1, source_target_pairs={{0,1},{1,16},{16,17},{17,32},{32,33},{33,48},{48,49},{49,64},{64,6... | collective-permute-start | bytes 983048 | tf_op jit(solution)/shard_map/ppermute | solution.py:34
  311.0 7.8 %collective-permute-start.35 = (bf16[4,512,512]{2,1,0:T(8,128)(2,1)S(1)}, bf16[4,512,512]{2,1,0:T(8,128)(2,1)S(1)}, u32[]{:S(2)}, u32[]{:S(2)}) collective-permute-start(bf16[4,512,512]{2,1,0:T(8,128)(2,1)S(1)} %get-tuple-element.32), channel_id=1, source_target_pairs={{0,8},{8,0},{1,9},{9,1},{2,10},{10,2},{3,11},{11,3},{4,12},{12,4},... | collective-permute-start | bytes 6291464 | tf_op jit(solution)/shard_map/ppermute | solution.py:20
  319.5 14.8 %collective-permute-start.38 = (bf16[512,512]{1,0:T(8,128)(2,1)S(1)}, bf16[512,512]{1,0:T(8,128)(2,1)S(1)}, u32[]{:S(2)}, u32[]{:S(2)}) collective-permute-start(bf16[512,512]{1,0:T(8,128)(2,1)S(1)} %get-tuple-element.38), channel_id=1, source_target_pairs={{0,4},{2,6},{4,0},{6,2},{1,5},{3,7},{5,1},{7,3},{8,12},{10,14},{12... | collective-permute-start | bytes 1572872 | tf_op jit(solution)/shard_map/ppermute | solution.py:20
  320.5 25.9 %collective-permute-start.37 = (bf16[512,512]{1,0:T(8,128)(2,1)S(1)}, bf16[512,512]{1,0:T(8,128)(2,1)S(1)}, u32[]{:S(2)}, u32[]{:S(2)}) collective-permute-start(bf16[512,512]{1,0:T(8,128)(2,1)S(1)} %get-tuple-element.39), channel_id=1, source_target_pairs={{0,6},{2,0},{4,2},{6,4},{1,7},{3,1},{5,3},{7,5},{8,14},{10,8},{12,... | collective-permute-start | bytes 1572872 | tf_op jit(solution)/shard_map/ppermute | solution.py:20
  323.4 23.0 %collective-permute-start.36 = (bf16[512,512]{1,0:T(8,128)(2,1)S(1)}, bf16[512,512]{1,0:T(8,128)(2,1)S(1)}, u32[]{:S(2)}, u32[]{:S(2)}) collective-permute-start(bf16[512,512]{1,0:T(8,128)(2,1)S(1)} %get-tuple-element.37), channel_id=1, source_target_pairs={{0,2},{2,4},{4,6},{6,0},{1,3},{3,5},{5,7},{7,1},{8,10},{10,12},{12... | collective-permute-start | bytes 1572872 | tf_op jit(solution)/shard_map/ppermute | solution.py:20
  346.8 14.0 %collective-permute-start.39 = (bf16[512,512]{1,0:T(8,128)(2,1)S(1)}, bf16[512,512]{1,0:T(8,128)(2,1)S(1)}, u32[]{:S(2)}, u32[]{:S(2)}) collective-permute-start(bf16[512,512]{1,0:T(8,128)(2,1)S(1)} %fusion.3), channel_id=1, source_target_pairs={{1,8},{8,1},{3,10},{10,3},{5,12},{12,5},{7,14},{14,7},{17,24},{24,... | collective-permute-start | bytes 1572872 | tf_op jit(solution)/shard_map/ppermute | solution.py:28
  (11 other events, 28.8 us)
Sparse Core Ops, SparseCore 0:
  9.7 88.3 all-gather.6
  120.4 96.3 all-gather.8
  219.0 54.1 all-gather.10
